TPU v7x, 256 devices: a whole 4x4x8 slice. The times are simulated.
256 devices in a mesh: seq: 32 (over y_hi, z, core), ch: 8 (over y_lo, x).
Axes of the slice: x: 4, y: 4 (y_hi: 2, y_lo: 2; y = y_hi * 2 + y_lo), z: 8, core: 2. Of those that a mesh axis runs over, the one named last changes fastest.
Arguments:
- layer_input: bfloat16 [12288, 4096], P('seq'), may hold values from -0.25 to 0.25
- value_proj: bfloat16 [12288, 4096], P('seq', 'ch'), may hold values from -4 to 4
- outer_gate: bfloat16 [12288, 4096], P('seq', 'ch'), may hold values from -1.5 to 1.5
- inner_gate: bfloat16 [12288, 4096], P('seq', 'ch'), may hold values from -4 to 4
- conv_output: bfloat16 [12288, 4096], P('seq', 'ch'), may hold values from -4 to 4
- upstream: bfloat16 [12288, 4096], P('seq'), may hold values from -6 to 6
- in_weight: bfloat16 [4096, 4096], P('seq', 'ch'), may hold values from -0.09375 to 0.09375
- out_weight: bfloat16 [4096, 4096], P('ch', 'seq'), may hold values from -0.09375 to 0.09375
- long_filter: bfloat16 [8, 512, 12288], P('ch', 'seq'), may hold values from -1.5 to 1.5
- short_filter: float32 [8, 512, 3], P('ch', 'seq'), may hold values from -5 to 5
Outputs:
- grad_input: bfloat16 [12288, 4096], P('seq', 'ch')
- grad_outer: bfloat16 [12288, 4096], P('seq', 'ch')
- grad_inner: bfloat16 [12288, 4096], P('seq', 'ch')
- grad_long: float32 [8, 512, 12288], P('ch', 'seq')
- grad_short: float32 [8, 512, 3], P('ch', 'seq')
- grad_inproj: float32 [4096, 4096], P('seq', 'ch')
- grad_outproj: float32 [4096, 4096], P('ch', 'seq')
All inputs are finite; a program needn't handle non-finite values.
Results may differ from a plain program's by a relative error of at most 0.02.
Values may be sent and summed in bfloat16 or wider, within the bound.
A program may use at most 128 MiB of HBM per device.

v0:
```python
import math

import jax
import jax.numpy as jnp
from jax import lax
from jax.sharding import PartitionSpec as P


def angle_table(rows_len, cols_len, modulus):
    rows = lax.broadcasted_iota(jnp.int32, (rows_len, cols_len), 0)
    cols = lax.broadcasted_iota(jnp.int32, (rows_len, cols_len), 1)
    phase = rows * cols % modulus
    angles = phase.astype(jnp.float32) * (2.0 * math.pi / modulus)
    return (jnp.cos(angles), jnp.sin(angles))


def make_tables(total):
    inner_len = math.gcd(total, 128)
    outer_len = total // inner_len
    cos_outer, sin_outer = angle_table(outer_len, outer_len, outer_len)
    cos_twist, sin_twist = angle_table(outer_len, inner_len, total)
    cos_inner, sin_inner = angle_table(inner_len, inner_len, inner_len)
    forward_outer = jnp.concatenate([cos_outer, -sin_outer], axis=1)
    forward_inner = jnp.concatenate(
        [
            jnp.concatenate([cos_inner, -sin_inner], axis=1),
            jnp.concatenate([sin_inner, cos_inner], axis=1),
        ],
        axis=0,
    )
    inverse_inner = jnp.concatenate(
        [
            jnp.concatenate([cos_inner, sin_inner], axis=1),
            jnp.concatenate([-sin_inner, cos_inner], axis=1),
        ],
        axis=0,
    )
    inverse_outer = jnp.concatenate([cos_outer, -sin_outer], axis=0)
    return (
        outer_len,
        inner_len,
        cos_twist,
        sin_twist,
        forward_outer,
        forward_inner,
        inverse_inner,
        inverse_outer,
    )


def forward_dft(signal, tables):
    (
        outer_len,
        inner_len,
        cos_twist,
        sin_twist,
        forward_outer,
        forward_inner,
        inverse_inner,
        inverse_outer,
    ) = tables
    chans, length = signal.shape
    padded = jnp.pad(signal, ((0, 0), (0, outer_len * inner_len - length)))
    blocks = padded.reshape(chans, outer_len, inner_len)
    first = jnp.einsum("cab,ak->ckb", blocks, forward_outer, precision=lax.Precision.HIGH)
    first_re = first[:, :outer_len]
    first_im = first[:, outer_len:]
    twist_re = first_re * cos_twist + first_im * sin_twist
    twist_im = first_im * cos_twist - first_re * sin_twist
    joined = jnp.concatenate([twist_re, twist_im], axis=2)
    spec = jnp.einsum("ckb,bm->ckm", joined, forward_inner, precision=lax.Precision.HIGHEST)
    return (spec[:, :, :inner_len], spec[:, :, inner_len:])


def inverse_dft(spec_re, spec_im, tables, length):
    (
        outer_len,
        inner_len,
        cos_twist,
        sin_twist,
        forward_outer,
        forward_inner,
        inverse_inner,
        inverse_outer,
    ) = tables
    chans = spec_re.shape[0]
    joined = jnp.concatenate([spec_re, spec_im], axis=2)
    middle = jnp.einsum("ckm,mb->ckb", joined, inverse_inner, precision=lax.Precision.HIGHEST)
    middle_re = middle[:, :, :inner_len]
    middle_im = middle[:, :, inner_len:]
    turned_re = middle_re * cos_twist - middle_im * sin_twist
    turned_im = middle_im * cos_twist + middle_re * sin_twist
    turned = jnp.concatenate([turned_re, turned_im], axis=1)
    signal = jnp.einsum("ckb,ka->cab", turned, inverse_outer, precision=lax.Precision.HIGHEST)
    signal = signal.reshape(chans, outer_len * inner_len) / float(outer_len * inner_len)
    return signal[:, :length]


def contract_rows(left, right):
    return lax.dot_general(
        left, right, (((0,), (0,)), ((), ())), preferred_element_type=jnp.float32
    )


def shards(
    layer_input,
    value_proj,
    outer_gate,
    inner_gate,
    conv_output,
    upstream,
    in_weight,
    out_weight,
    long_filter,
    short_filter,
):
    in_whole, out_whole = (
        lax.all_gather(in_weight, "seq", axis=0, tiled=True),
        lax.all_gather(out_weight, "seq", axis=1, tiled=True),
    )
    product = (outer_gate.astype(jnp.float32) * conv_output.astype(jnp.float32)).astype(
        jnp.bfloat16
    )
    grad_mix = lax.dot_general(
        upstream, out_whole, (((1,), (1,)), ((), ())), preferred_element_type=jnp.float32
    )
    grad_outer = (grad_mix * conv_output.astype(jnp.float32)).astype(jnp.bfloat16)
    grad_conv = (grad_mix * outer_gate.astype(jnp.float32)).astype(jnp.bfloat16)
    value_cols, inner_cols, conv_cols = (
        lax.all_to_all(value_proj, "seq", split_axis=1, concat_axis=0, tiled=True),
        lax.all_to_all(inner_gate, "seq", split_axis=1, concat_axis=0, tiled=True),
        lax.all_to_all(grad_conv, "seq", split_axis=1, concat_axis=0, tiled=True),
    )
    length = value_cols.shape[0]
    values = value_cols.T.astype(jnp.float32)
    gates = inner_cols.T.astype(jnp.float32)
    back = conv_cols.T.astype(jnp.float32)
    chans = back.shape[0]
    taps = short_filter[0]
    tap_count = taps.shape[1]
    past = [jnp.pad(values, ((0, 0), (j, 0)))[:, :length] for j in range(tap_count)]
    smooth = taps[:, 0:1] * past[0]
    for j in range(1, tap_count):
        smooth = smooth + taps[:, j : j + 1] * past[j]
    mixed = (gates * smooth).astype(jnp.bfloat16)
    tables = make_tables(2 * length)
    signals = jnp.concatenate(
        [back, long_filter[0].astype(jnp.float32), mixed.astype(jnp.float32)], axis=0
    )
    all_re, all_im = forward_dft(signals, tables)
    back_re = all_re[:chans]
    back_im = all_im[:chans]
    other_re = all_re[chans:]
    other_im = all_im[chans:]
    pair_re = jnp.concatenate([back_re, back_re], axis=0)
    pair_im = jnp.concatenate([back_im, back_im], axis=0)
    results = inverse_dft(
        pair_re * other_re + pair_im * other_im,
        pair_im * other_re - pair_re * other_im,
        tables,
        length,
    )
    grad_mixed = results[:chans]
    grad_long = results[chans:]
    grad_inner_cols = (grad_mixed * smooth).astype(jnp.bfloat16)
    grad_smooth = grad_mixed * gates
    grad_value_cols = taps[:, 0:1] * grad_smooth
    for j in range(1, tap_count):
        grad_value_cols = (
            grad_value_cols + taps[:, j : j + 1] * jnp.pad(grad_smooth, ((0, 0), (0, j)))[:, j:]
        )
    grad_value_cols = grad_value_cols.astype(jnp.bfloat16)
    grad_taps = jnp.stack(
        [jnp.sum(grad_smooth * past[j], axis=1) for j in range(tap_count)], axis=1
    )
    grad_inner, grad_value = (
        lax.all_to_all(grad_inner_cols.T, "seq", split_axis=0, concat_axis=1, tiled=True),
        lax.all_to_all(grad_value_cols.T, "seq", split_axis=0, concat_axis=1, tiled=True),
    )
    partial_input = lax.dot_general(
        grad_value, in_whole, (((1,), (1,)), ((), ())), preferred_element_type=jnp.float32
    )
    grad_input = lax.psum_scatter(partial_input, "ch", scatter_dimension=1, tiled=True).astype(
        jnp.bfloat16
    )
    in_term = contract_rows(layer_input, grad_value)
    out_term = contract_rows(product, upstream)
    grad_inproj, grad_outproj = (
        lax.psum_scatter(
            in_term.astype(jnp.bfloat16), "seq", scatter_dimension=0, tiled=True
        ).astype(jnp.float32),
        lax.psum_scatter(
            out_term.astype(jnp.bfloat16), "seq", scatter_dimension=1, tiled=True
        ).astype(jnp.float32),
    )
    return (
        grad_input,
        grad_outer,
        grad_inner,
        grad_long[None],
        grad_taps[None],
        grad_inproj,
        grad_outproj,
    )


def solution(mesh):
    in_specs = (
        P("seq", None),
        P("seq", "ch"),
        P("seq", "ch"),
        P("seq", "ch"),
        P("seq", "ch"),
        P("seq", None),
        P("seq", "ch"),
        P("ch", "seq"),
        P("ch", "seq", None),
        P("ch", "seq", None),
    )
    out_specs = (
        P("seq", "ch"),
        P("seq", "ch"),
        P("seq", "ch"),
        P("ch", "seq", None),
        P("ch", "seq", None),
        P("seq", "ch"),
        P("ch", "seq"),
    )
    return jax.shard_map(shards, mesh=mesh, in_specs=in_specs, out_specs=out_specs, check_vma=False)
```

profile of v0, /device:TPU:15, one launch (start us, length us, event | category | flops | bytes accessed | tf_op | source)
XLA Modules:
  0.0 539.7 jit_solution(60527531413574171)
XLA Ops:
  7.2 0.7 all-gather.3.cloned.1.call-update
  8.0 0.7 all-gather.5.cloned.1.call-update
  8.7 1.9 copy.47
  10.6 11.0 %all-to-all-start.2 = ((bf16[384,32,16]{0,2,1:T(8,128)(2,1)}), bf16[384,32,16]{0,2,1:T(8,128)(2,1)S(1)}, u32[]{:S(2)}, u32[]{:S(2)}) async-start(bf16[384,32,16]{0,2,1:T(8,128)(2,1)} %bitcast.10), calls=%async_computation.2 | async-start | bytes 786432 | tf_op jit(solution)/shard_map/all_to_all | solution.py:130
  21.7 5.5 %convolution_convert_fusion = bf16[512,4096]{1,0:T(8,128)(2,1)} fusion(bf16[384,4096]{1,0:T(8,128)(2,1)S(1)} %copy-done, bf16[384,512]{1,0:T(8,128)(2,1)} %param.14, bf16[384,512]{1,0:T(8,128)(2,1)} %param.12), kind=kOutput, calls=%fused_computation.12 | convolution fusion | flops 1613496320 | bytes 8126464 | tf_op jit(solution)/shard_map/dot_general | solution.py:100
  27.1 6.5 %copy.59 = bf16[512,4096]{0,1:T(8,128)(2,1)} copy(bf16[512,4096]{1,0:T(8,128)(2,1)} %convolution_convert_fusion) | data formatting | bytes 8388608
  33.6 1.9 copy.45
  35.5 0.9 fusion.71
  36.5 1.5 all-to-all-done.2
  37.9 8.4 %all-to-all-start.1 = ((bf16[384,32,16]{0,2,1:T(8,128)(2,1)}), bf16[384,32,16]{0,2,1:T(8,128)(2,1)}, u32[]{:S(2)}, u32[]{:S(2)}) async-start(bf16[384,32,16]{0,2,1:T(8,128)(2,1)} %bitcast.7), calls=%async_computation.1 | async-start | bytes 786432 | tf_op jit(solution)/shard_map/all_to_all | solution.py:131
  46.3 0.9 fusion.73
  47.2 1.1 fusion.62
  48.3 0.8 sine_negate_fusion
  49.2 1.1 convert_bitcast_fusion
  50.2 1.0 copy.66
  51.2 11.4 %all-to-all-done.1 = bf16[384,32,16]{0,2,1:T(8,128)(2,1)} async-done(((bf16[384,32,16]{0,2,1:T(8,128)(2,1)}), bf16[384,32,16]{0,2,1:T(8,128)(2,1)}, u32[]{:S(2)}, u32[]{:S(2)}) %all-to-all-start.1) | async-done | bytes 393248 | tf_op jit(solution)/shard_map/all_to_all | solution.py:131
  62.6 1.0 convert_bitcast_fusion.1
  63.7 0.9 copy.65
  64.6 41.6 %all-gather.3.cloned.1.call-done = bf16[512,4096]{1,0:T(8,128)(2,1)} async-done(((bf16[512,128]{1,0:T(8,128)(2,1)}), bf16[512,4096]{1,0:T(8,128)(2,1)}) %all-gather.3.cloned.1.call-update) | async-done | bytes 4194320 | tf_op jit(solution)/shard_map/all_gather | solution.py:119
  106.2 5.1 fusion.34
  111.3 2.0 copy.43
  113.3 5.6 %all-to-all-start = ((bf16[384,32,16]{0,2,1:T(8,128)(2,1)}), bf16[384,32,16]{0,2,1:T(8,128)(2,1)S(1)}, u32[]{:S(2)}, u32[]{:S(2)}) async-start(bf16[384,32,16]{0,2,1:T(8,128)(2,1)} %bitcast.3), calls=%async_computation | async-start | bytes 786432 | tf_op jit(solution)/shard_map/all_to_all | solution.py:132
  119.4 3.4 fusion.36
  122.8 14.7 %all-to-all-done = bf16[384,32,16]{0,2,1:T(8,128)(2,1)S(1)} async-done(((bf16[384,32,16]{0,2,1:T(8,128)(2,1)}), bf16[384,32,16]{0,2,1:T(8,128)(2,1)S(1)}, u32[]{:S(2)}, u32[]{:S(2)}) %all-to-all-start) | async-done | bytes 393248 | tf_op jit(solution)/shard_map/all_to_all | solution.py:132
  138.4 2.8 convolution_bitcast_fusion
  141.3 3.6 multiply_add_fusion
  144.9 10.6 %fusion = f32[48,192,256]{2,1,0:T(8,128)S(1)} fusion(f32[48,192,128]{2,1,0:T(8,128)} %get-tuple-element.44, f32[48,192,128]{2,1,0:T(8,128)S(1)} %get-tuple-element.43, f32[128,128]{1,0:T(8,128)S(1)} %copy-done.11, f32[128,128]{1,0:T(8,128)S(1)} %copy-done.9, f32[128,128]{1,0:T(8,128)S(1)} %copy-done.13), kind=kOutput, calls=%fused_computation | convolution fusion | flops 7250313216 | bytes 19070976 | tf_op jit(solution)/shard_map/ckb,bm->ckm/dot_general | solution.py:71
  155.9 1.1 fusion.18
  157.1 5.4 fusion.4
  162.5 0.7 multiply_subtract_fusion.1
  163.2 5.6 %fusion.25 = f32[192,32,128]{2,0,1:T(8,128)S(1)} fusion(f32[32,192,128]{2,1,0:T(8,128)S(1)} %get-tuple-element.48, f32[32,192,128]{2,1,0:T(8,128)S(1)} %get-tuple-element.47, f32[192,192]{1,0:T(8,128)S(1)} %get-tuple-element.60, f32[192,192]{1,0:T(8,128)S(1)} %get-tuple-element.61), kind=kOutput, calls=%fused_computation.36 | convolution fusion | flops 3626311680 | bytes 9732096 | tf_op jit(solution)/shard_map/ckb,ka->cab/dot_general | solution.py:94
  168.8 2.0 copy.73
  170.9 2.0 slice_bitcast_fusion
  173.4 21.6 %all_to_all.77 = bf16[32,384,16]{1,2,0:T(8,128)(2,1)S(1)} all-to-all(bf16[32,384,16]{1,2,0:T(8,128)(2,1)S(1)} %bitcast.108), channel_id=1, replica_groups=mesh['seq'=32,'ch'=8] {'seq'}, dimensions={0} | all-to-all | bytes 786432 | tf_op jit(solution)/shard_map/all_to_all | solution.py:178
  195.0 4.3 fusion.12
  199.3 6.5 %copy.57 = bf16[4096,512]{1,0:T(8,128)(2,1)} copy(bf16[4096,512]{0,1:T(8,128)(2,1)} %fusion.12) | data formatting | bytes 8388608
  205.9 6.7 %fusion.79 = f32[384,4096]{1,0:T(8,128)} fusion(bf16[384,512]{0,1:T(8,128)(2,1)S(1)} %bitcast.110, bf16[4096,512]{1,0:T(8,128)(2,1)} %all-gather.5.cloned.1.call-done), kind=kOutput, calls=%fused_computation.123 | convolution fusion | flops 1610612736 | bytes 10878976 | tf_op jit(solution)/shard_map/dot_general | solution.py:180
  212.6 0.8 copy.74
  213.4 5.4 %all-to-all-start.4 = ((bf16[32,384,16]{1,2,0:T(8,128)(2,1)}), bf16[32,384,16]{1,2,0:T(8,128)(2,1)S(1)}, u32[]{:S(2)}, u32[]{:S(2)}) async-start(bf16[32,384,16]{1,2,0:T(8,128)(2,1)} %bitcast.104), calls=%async_computation.5 | async-start | bytes 786432 | tf_op jit(solution)/shard_map/all_to_all | solution.py:177
  218.9 103.4 %reduce-scatter.12.cloned.1.call-done = bf16[128,512]{1,0:T(8,128)(2,1)} async-done(((bf16[4096,512]{1,0:T(8,128)(2,1)}), bf16[128,512]{1,0:T(8,128)(2,1)}) %reduce-scatter.12.cloned.1.call-update) | async-done | bytes 131088
  322.3 1.7 copy.60
  323.9 1.6 convert_element_type.171
  326.1 0.9 copy.52
  327.1 125.7 %reduce-scatter.10.cloned.1.call-done = bf16[128,512]{1,0:T(8,128)(2,1)} async-done(((bf16[4096,512]{1,0:T(8,128)(2,1)}), bf16[128,512]{1,0:T(8,128)(2,1)}) %reduce-scatter.10.cloned.1.call-update) | async-done | bytes 131088
  452.8 1.0 copy.58
  453.8 0.8 copy.54
  454.6 76.4 %reduce-scatter.8.cloned.1.call-done = f32[384,512]{1,0:T(8,128)} async-done(((f32[384,4096]{1,0:T(8,128)}), f32[384,512]{1,0:T(8,128)}) %reduce-scatter.8.cloned.1.call-update) | async-done | bytes 786448 | tf_op jit(solution)/shard_map/reduce_scatter | solution.py:183
  531.0 1.9 convert_element_type.162
  (60 shorter events, 3.2 us)
Async XLA Ops:
  7.2 14.5 %copy-start = (bf16[384,4096]{1,0:T(8,128)(2,1)S(1)}, bf16[384,4096]{1,0:T(8,128)(2,1)}, u32[]{:S(2)}) copy-start(bf16[384,4096]{1,0:T(8,128)(2,1)} %param.15) | copy-start | bytes 9437188
  7.2 99.0 %all-gather.3.cloned.1.call-start = ((), (), s32[]{:S(2)}) async-start(), calls=%async_computation.8 | async-start | bytes 4325376 | tf_op jit(solution)/shard_map/all_gather | solution.py:119
  7.9 198.0 %all-gather.5.cloned.1.call-start = ((), (), s32[]{:S(2)}) async-start(), calls=%async_computation.9 | async-start | bytes 4325376 | tf_op jit(solution)/shard_map/all_gather | solution.py:118
  10.6 27.3 %all-to-all-start.2 = ((bf16[384,32,16]{0,2,1:T(8,128)(2,1)}), bf16[384,32,16]{0,2,1:T(8,128)(2,1)S(1)}, u32[]{:S(2)}, u32[]{:S(2)}) async-start(bf16[384,32,16]{0,2,1:T(8,128)(2,1)} %bitcast.10), calls=%async_computation.2 | async-start | bytes 786432 | tf_op jit(solution)/shard_map/all_to_all | solution.py:130
  21.6 300.6 %reduce-scatter.12.cloned.1.call-start = ((), (), s32[]{:S(2)}) async-start(), calls=%async_computation.12 | async-start | bytes 4325376
  33.6 13.6 %copy-start.18 = (f32[1,16,3]{1,0,2:T(1,128)S(1)}, f32[1,16,3]{1,0,2:T(1,128)}, u32[]{:S(2)}) copy-start(f32[1,16,3]{1,0,2:T(1,128)} %param.19) | copy-start | bytes 580
  37.9 9.3 %copy-start.5 = (bf16[384,32,16]{0,2,1:T(8,128)(2,1)}, bf16[384,32,16]{0,2,1:T(8,128)(2,1)S(1)}, u32[]{:S(2)}) copy-start(bf16[384,32,16]{0,2,1:T(8,128)(2,1)S(1)} %all-to-all-done.2) | copy-start | bytes 1179652
  37.9 24.7 %all-to-all-start.1 = ((bf16[384,32,16]{0,2,1:T(8,128)(2,1)}), bf16[384,32,16]{0,2,1:T(8,128)(2,1)}, u32[]{:S(2)}, u32[]{:S(2)}) async-start(bf16[384,32,16]{0,2,1:T(8,128)(2,1)} %bitcast.7), calls=%async_computation.1 | async-start | bytes 786432 | tf_op jit(solution)/shard_map/all_to_all | solution.py:131
  111.3 26.2 %copy-start.15 = (bf16[1,16,12288]{2,1,0:T(8,128)(2,1)S(1)}, bf16[1,16,12288]{2,1,0:T(8,128)(2,1)}, u32[]{:S(2)}) copy-start(bf16[1,16,12288]{2,1,0:T(8,128)(2,1)} %param.18) | copy-start | bytes 1179652
  113.3 24.2 %all-to-all-start = ((bf16[384,32,16]{0,2,1:T(8,128)(2,1)}), bf16[384,32,16]{0,2,1:T(8,128)(2,1)S(1)}, u32[]{:S(2)}, u32[]{:S(2)}) async-start(bf16[384,32,16]{0,2,1:T(8,128)(2,1)} %bitcast.3), calls=%async_computation | async-start | bytes 786432 | tf_op jit(solution)/shard_map/all_to_all | solution.py:132
  118.8 333.9 %reduce-scatter.10.cloned.1.call-start = ((), (), s32[]{:S(2)}) async-start(), calls=%async_computation.11 | async-start | bytes 4325376
  138.4 2.8 copy-start.6
  138.4 2.8 copy-start.7
  141.3 3.7 copy-start.9
  141.3 3.7 copy-start.11
  141.3 3.7 copy-start.13
  155.9 1.1 copy-start.10
  155.9 1.1 copy-start.12
  155.9 1.1 copy-start.14
  157.1 5.4 copy-start.8
  168.8 2.1 copy-start.2
  168.8 2.1 copy-start.3
  168.8 2.1 copy-start.4
  170.9 24.2 %copy-start.19 = (bf16[384,4096]{1,0:T(8,128)(2,1)S(1)}, bf16[384,4096]{1,0:T(8,128)(2,1)}, u32[]{:S(2)}) copy-start(bf16[384,4096]{1,0:T(8,128)(2,1)} %param.10) | copy-start | bytes 9437188
  205.8 325.1 %reduce-scatter.8.cloned.1.call-start = ((), (), s32[]{:S(2)}) async-start(), calls=%async_computation.10 | async-start | bytes 7077888 | tf_op jit(solution)/shard_map/reduce_scatter | solution.py:183
  212.6 113.0 %copy-start.16 = (f32[16]{0:T(128)S(1)}, f32[16]{0:T(128)}, u32[]{:S(2)}) copy-start(f32[16]{0:T(128)} %get-tuple-element.52) | copy-start | bytes 196
  212.6 113.0 %copy-start.17 = (f32[16]{0:T(128)S(1)}, f32[16]{0:T(128)}, u32[]{:S(2)}) copy-start(f32[16]{0:T(128)} %get-tuple-element.53) | copy-start | bytes 196
  212.6 320.3 %copy-start.1 = (bf16[384,4096]{1,0:T(8,128)(2,1)S(1)}, bf16[384,4096]{1,0:T(8,128)(2,1)}, u32[]{:S(2)}) copy-start(bf16[384,4096]{1,0:T(8,128)(2,1)} %param.15) | copy-start | bytes 9437188
  213.4 112.7 %all-to-all-start.4 = ((bf16[32,384,16]{1,2,0:T(8,128)(2,1)}), bf16[32,384,16]{1,2,0:T(8,128)(2,1)S(1)}, u32[]{:S(2)}, u32[]{:S(2)}) async-start(bf16[32,384,16]{1,2,0:T(8,128)(2,1)} %bitcast.104), calls=%async_computation.5 | async-start | bytes 786432 | tf_op jit(solution)/shard_map/all_to_all | solution.py:177
Sparse Core Ops, SparseCore 0:
  10.6 95.5 all-gather.2
  109.0 88.0 all-gather.4
  201.3 120.9 reduce-scatter.11
  326.9 125.7 reduce-scatter.9
  455.2 75.7 reduce-scatter.7
where the time goes:
time: 551 us; the launch traced here: 540 us
  waiting for transfers between devices  376 us (68%)
  matrix products  45.9 us (8%)
  starting transfers between devices  31.1 us (6%)
  local copies, waits for them, and re-layouts  29.6 us (5%)
  blocking collectives  21.6 us (4%)
  other arithmetic  20.9 us (4%)
  between operations  14.4 us (3%)
    unnamed x7, waiting for transfers between devices  231 us
    reduce_scatter x1, waiting for transfers between devices, shards(): lax.psum_scatter(partial_input, 'ch', scatter_dimension=1, tiled=True)  76.4 us
    all_gather x1, waiting for transfers between devices, shards(): lax.all_gather(out_weight, 'seq', axis=1, tiled=True)  41.6 us
    unnamed x52, local copies, waits for them, and re-layouts  24.5 us
    all_to_all x1, blocking collectives, shards(): lax.all_to_all(grad_value_cols.T, 'seq', split_axis=0, concat_axis=1, til...  21.6 us
    all_to_all x1, waiting for transfers between devices, shards(): lax.all_to_all(grad_conv, 'seq', split_axis=1, concat_axis=0, tiled=True)  14.7 us
    all_to_all x1, waiting for transfers between devices, shards(): lax.all_to_all(inner_gate, 'seq', split_axis=1, concat_axis=0, tiled=True)  11.4 us
    all_to_all x1, starting transfers between devices, shards(): lax.all_to_all(value_proj, 'seq', split_axis=1, concat_axis=0, tiled=True)  11 us
  transfers between devices with their start and end apart: 9, of which 7 were waited for; matrix products, arithmetic and copies ran while one was open for 17% of the time, Pallas kernels for 0%

commit v1 on v0

v1 whole, which is shorter than its diff:
```python
import math

import ml_dtypes
import numpy as np
import jax
import jax.numpy as jnp
from jax import lax
from jax.experimental import pallas as pl
from jax.experimental.pallas import tpu as pltpu
from jax.sharding import PartitionSpec as P

MESH = pl.DeviceIdType.MESH
F32 = jnp.float32
BF16 = jnp.bfloat16
N_SEQ = 32
ROWS = 384
CHANS = 512
MINE = 16
WIDE = 128
LENGTH = N_SEQ * ROWS
OUTER = LENGTH // WIDE
SIGNS = (1, -1)


def split_table(table):
    high = table.astype(ml_dtypes.bfloat16)
    low = (table - high.astype(np.float64)).astype(ml_dtypes.bfloat16)
    return high, low


def dft_tables():
    order = np.array([3 * s + q for q in range(3) for s in range(N_SEQ)])
    a = np.arange(OUTER)
    b = np.arange(WIDE)
    k1 = np.arange(OUTER)
    k2 = np.arange(WIDE)
    turn = np.pi / (2 * LENGTH)
    outer = 2 * np.pi * np.outer(k1, a) / OUTER + turn * WIDE * a[None, :]
    twist = 2 * np.pi * np.outer(k1, b) / LENGTH + turn * b[None, :]
    inner = 2 * np.pi * np.outer(b, k2) / WIDE
    first = np.concatenate([np.cos(outer), -np.sin(outer)], axis=0)[:, order]
    co, si = np.cos(inner), np.sin(inner)
    second = np.block([[co, -si], [si, co]])
    third = np.block([[co, si], [-si, co]])
    last = np.concatenate([np.cos(outer).T, -np.sin(outer).T], axis=1) / LENGTH
    first_h, first_l = split_table(first)
    second_h, second_l = split_table(second)
    third_h, third_l = split_table(third)
    perm_h, perm_l = split_table(last[order])
    last_h, last_l = split_table(last)
    return (
        np.concatenate([first_h, first_l], axis=0),
        second_h,
        second_l,
        third_h,
        third_l,
        np.stack([perm_h, perm_l, last_h, last_l]),
        np.cos(twist).astype(np.float32),
        np.sin(twist).astype(np.float32),
    )


def remote(src, dst, send, recv, axis, index):
    return pltpu.make_async_remote_copy(
        src_ref=src,
        dst_ref=dst,
        send_sem=send,
        recv_sem=recv,
        device_id={axis: index},
        device_id_type=MESH,
    )


def place():
    s = lax.axis_index("seq")
    return s, s // 16, (s // 2) % 8, s % 2


def at_seq(y, z, c):
    return y * 16 + z * 2 + c


def greet_all(barrier, s):
    def body(i, _):
        pl.semaphore_signal(
            barrier, inc=1, device_id={"seq": (s + i) % N_SEQ}, device_id_type=MESH
        )
        return 0

    lax.fori_loop(1, N_SEQ, body, 0)


def exchange(source_of, target, sends, recvs, s):
    def body(i, _):
        dst = (s + i) % N_SEQ
        remote(source_of(dst), target, sends.at[i], recvs.at[i], "seq", dst).start()
        return 0

    lax.fori_loop(1, N_SEQ, body, 0)


def arrived(landing_of, sends, recvs, s):
    def body(i, _):
        src = (s + N_SEQ - i) % N_SEQ
        here = landing_of(src)
        remote(here, here, sends.at[i], recvs.at[i], "seq", src).wait_recv()
        return 0

    lax.fori_loop(1, N_SEQ, body, 0)


def left(piece, sends, recvs, s):
    def body(i, _):
        remote(piece, piece, sends.at[i], recvs.at[i], "seq", (s + i) % N_SEQ).wait_send()
        return 0

    lax.fori_loop(1, N_SEQ, body, 0)


class Gather:
    sems = [
        pltpu.SemaphoreType.DMA((2, 4, 2)),
        pltpu.SemaphoreType.DMA((2, 4, 2)),
        pltpu.SemaphoreType.DMA((2, 8)),
        pltpu.SemaphoreType.DMA((2, 8)),
        pltpu.SemaphoreType.DMA((2,)),
    ]

    def __init__(self, shard, whole, sems, at):
        self.shard, self.whole, self.at = shard, whole, at
        self.zs, self.zr, self.cs, self.cr, self.ys = sems
        self.started = []

    def slot(self, sub, o, other=False):
        _, y, z, c = self.at
        yy = 1 - y if sub else y
        return at_seq(yy, (z + o + 8) % 8, 1 - c if other else c)

    def go(self, copy):
        copy.start()
        self.started.append(copy)

    def source(self, sub, o):
        if sub == 0 and o == 0:
            return self.shard
        return self.whole.at[self.slot(sub, o)]

    def hop(self, di, d, sub):
        _, y, z, c = self.at
        o = -SIGNS[di] * (d - 1)
        there = at_seq(y, (z + SIGNS[di] + 8) % 8, c)
        self.go(
            remote(
                self.source(sub, o),
                self.whole.at[self.slot(sub, o)],
                self.zs.at[di, d - 1, sub],
                self.zr.at[di, d - 1, sub],
                "seq",
                there,
            )
        )

    def share(self, sub, o):
        _, y, z, c = self.at
        self.go(
            remote(
                self.source(sub, o),
                self.whole.at[self.slot(sub, o)],
                self.cs.at[sub, o % 8],
                self.cr.at[sub, o % 8],
                "seq",
                at_seq(y, z, 1 - c),
            )
        )

    def pair(self):
        _, y, z, c = self.at
        return remote(
            self.shard,
            self.whole.at[self.slot(0, 0)],
            self.ys.at[0],
            self.ys.at[1],
            "seq",
            at_seq(1 - y, z, c),
        )

    @staticmethod
    def travels(di, d, sub):
        return d < 4 or (d == 4 and sub == di)

    def begin(self):
        self.hop(0, 1, 0)
        self.hop(1, 1, 0)
        self.go(self.pair())
        self.share(0, 0)
        self.whole[self.slot(0, 0)] = self.shard[...]

    def steps(self):
        self.pair().wait_recv()
        self.hop(0, 1, 1)
        self.hop(1, 1, 1)
        self.share(1, 0)
        yield
        for d in range(1, 5):
            for sub in range(2):
                for di in range(2):
                    if not self.travels(di, d, sub):
                        continue
                    o = -SIGNS[di] * d
                    here = self.whole.at[self.slot(sub, o)]
                    remote(
                        here,
                        here,
                        self.zs.at[di, d - 1, sub],
                        self.zr.at[di, d - 1, sub],
                        "seq",
                        self.at[0],
                    ).wait_recv()
                    if self.travels(di, d + 1, sub):
                        self.hop(di, d + 1, sub)
                    self.share(sub, o)
                yield

    def ready(self, sub, o):
        _, y, z, c = self.at
        here = self.whole.at[self.slot(sub, o, other=True)]
        remote(
            here, here, self.cs.at[sub, o % 8], self.cr.at[sub, o % 8], "seq", self.at[0]
        ).wait_recv()
        yy = 1 - y if sub else y
        return yy * 8 + (z + o + 8) % 8

    def end(self):
        for copy in self.started:
            copy.wait_send()


class Scatter:
    @staticmethod
    def scratch():
        return [
            pltpu.VMEM((2, 8, CHANS, WIDE), BF16),
            pltpu.VMEM((2, 8, CHANS, WIDE), BF16),
            pltpu.VMEM((2, 8, CHANS, WIDE), BF16),
            pltpu.VMEM((2, 4, 2, CHANS, WIDE), BF16),
            pltpu.VMEM((2, CHANS, WIDE), BF16),
            pltpu.SemaphoreType.DMA((2, 4, 2)),
            pltpu.SemaphoreType.DMA((2, 4, 2)),
            pltpu.SemaphoreType.DMA((2, 8)),
            pltpu.SemaphoreType.DMA((2, 8)),
            pltpu.SemaphoreType.DMA((2,)),
        ]

    def __init__(self, scratch, at):
        self.at = at
        self.own, self.tx, self.rx, self.zrx, self.yrx = scratch[:5]
        self.zs, self.zr, self.cs, self.cr, self.ys = scratch[5:]
        self.started = []

    def go(self, copy):
        copy.start()
        self.started.append(copy)

    def hand(self, sub, o):
        _, y, z, c = self.at
        return remote(
            self.tx.at[sub, o],
            self.rx.at[sub, o],
            self.cs.at[sub, o],
            self.cr.at[sub, o],
            "seq",
            at_seq(y, z, 1 - c),
        )

    def partials(self, left_t, right):
        _, y, z, c = self.at

        def body(i, _):
            o = (4 + (1 - 2 * (i % 2)) * ((i + 1) // 2) + 8) % 8
            for sub in range(2):
                yy = 1 - y if sub else y
                m = yy * 8 + (z + o) % 8
                cols = pl.ds(pl.multiple_of(m * 2 * WIDE, 2 * WIDE), 2 * WIDE)
                part = jnp.dot(left_t[...], right[:, cols], preferred_element_type=F32)
                low = part[:, :WIDE].astype(BF16)
                high = part[:, WIDE:].astype(BF16)
                self.own[sub, o] = jnp.where(c == 0, low, high)
                self.tx[sub, o] = jnp.where(c == 0, high, low)
                self.hand(sub, o).start()
            return 0

        lax.fori_loop(0, 8, body, 0)

    def hop(self, di, d, sub):
        _, y, z, c = self.at
        o = (SIGNS[di] * d) % 8
        there = at_seq(y, (z + SIGNS[di] + 8) % 8, c)
        return remote(
            self.own.at[sub, o],
            self.zrx.at[di, d - 1, sub],
            self.zs.at[di, d - 1, sub],
            self.zr.at[di, d - 1, sub],
            "seq",
            there,
        )

    def pair(self):
        _, y, z, c = self.at
        return remote(
            self.yrx.at[0],
            self.yrx.at[1],
            self.ys.at[0],
            self.ys.at[1],
            "seq",
            at_seq(1 - y, z, c),
        )

    def both(self, sub, o):
        self.hand(sub, o).wait_recv()
        return self.own[sub, o].astype(F32) + self.rx[sub, o].astype(F32)

    def steps(self):
        for d in range(4, 0, -1):
            for sub in range(2):
                for di in range(2):
                    if not Gather.travels(di, d, sub):
                        continue
                    o = (SIGNS[di] * d) % 8
                    total = self.both(sub, o)
                    if Gather.travels(di, d + 1, sub):
                        self.hop(di, d + 1, sub).wait_recv()
                        total = total + self.zrx[di, d, sub].astype(F32)
                    self.own[sub, o] = total.astype(BF16)
                    self.go(self.hop(di, d, sub))
                yield

    def finish(self, out):
        def total(sub):
            value = self.both(sub, 0)
            for di in range(2):
                self.hop(di, 1, sub).wait_recv()
                value = value + self.zrx[di, 0, sub].astype(F32)
            return value

        self.yrx[0] = total(1).astype(BF16)
        self.pair().start()
        out[...] = total(0)
        self.pair().wait_recv()
        out[...] += self.yrx[1].astype(F32)
        self.pair().wait_send()
        for copy in self.started:
            copy.wait_send()

        def body(i, _):
            for sub in range(2):
                self.hand(sub, i).wait_send()
            return 0

        lax.fori_loop(0, 8, body, 0)


def sixteen(index):
    return pl.ds(pl.multiple_of(index * MINE, MINE), MINE)


def front_kernel(
    out_shard, upstream, outer_gate, conv_output, value, gate, taps,
    grad_outer, product_t, conv_rx, mix_rx, padded, all_taps,
    whole, acc, conv_t, mix_t, halo, taps_rx,
    gather_0, gather_1, gather_2, gather_3, gather_4,
    halo_sem, taps_s, taps_r, mix_s, mix_r, conv_s, conv_r,
):
    at = place()
    s, y, z, c = at
    barrier = pltpu.get_barrier_semaphore()
    greet_all(barrier, s)
    pl.semaphore_wait(barrier, N_SEQ - 1)

    ring = Gather(out_shard, whole, (gather_0, gather_1, gather_2, gather_3, gather_4), at)
    ring.begin()
    edge = remote(
        value.at[pl.ds(ROWS - 16, 16)],
        halo,
        halo_sem.at[0],
        halo_sem.at[1],
        "seq",
        (s + 1) % N_SEQ,
    )
    edge.start()
    exchange(lambda d: taps, taps_rx.at[s], taps_s, taps_r, s)
    taps_rx[s] = taps[...]
    step = ring.steps()

    for r in range(0, ROWS, WIDE):
        rows = pl.ds(r, WIDE)
        product = outer_gate[rows, :].astype(F32) * conv_output[rows, :].astype(F32)
        product_t[:, rows] = product.T.astype(BF16)
        padded[pl.ds(8 + r, WIDE), :] = value[rows, :].astype(F32)
    next(step)

    arrived(lambda d: taps_rx.at[d], taps_s, taps_r, s)
    for g in range(4):
        tile = taps_rx[8 * g]
        for i in range(1, 8):
            tile = tile + taps_rx[8 * g + i]
        all_taps[:, pl.ds(g * WIDE, WIDE)] = tile
    edge.wait_recv()
    padded[pl.ds(0, 8), :] = jnp.where(s == 0, 0.0, halo[...].astype(F32)[8:, :])
    next(step)
    for r in range(0, ROWS, WIDE):
        smooth = all_taps[pl.ds(0, 1), :] * padded[pl.ds(8 + r, WIDE), :]
        for j in range(1, 3):
            smooth = smooth + all_taps[pl.ds(j, 1), :] * padded[pl.ds(8 + r - j, WIDE), :]
        mixed = gate[pl.ds(r, WIDE), :].astype(F32) * smooth
        mix_t[:, pl.ds(r, WIDE)] = mixed.T.astype(BF16)
    next(step)
    exchange(lambda d: mix_t.at[sixteen(d)], mix_rx.at[sixteen(s)], mix_s, mix_r, s)
    mix_rx[sixteen(s), :] = mix_t[sixteen(s), :]

    def multiply(sub, o, first=False):
        m = ring.ready(sub, o)
        cols = pl.ds(pl.multiple_of(m * 2 * WIDE, 2 * WIDE), 2 * WIDE)
        shards = jnp.concatenate([whole[2 * m], whole[2 * m + 1]], axis=1)
        part = lax.dot_general(
            upstream[:, cols], shards, (((1,), (1,)), ((), ())), preferred_element_type=F32
        )
        acc[...] = part if first else acc[...] + part

    multiply(0, 0, True)
    multiply(1, 0)
    for d in range(2, 5):
        next(step)
        multiply(0, d - 1)
        multiply(0, 1 - d)
        next(step)
        multiply(1, d - 1)
        multiply(1, 1 - d)
    for _ in step:
        pass
    multiply(0, 4)
    multiply(1, 4)

    for r in range(0, ROWS, WIDE):
        rows = pl.ds(r, WIDE)
        conv = acc[rows, :] * outer_gate[rows, :].astype(F32)
        conv_t[:, rows] = conv.T.astype(BF16)
    exchange(lambda d: conv_t.at[sixteen(d)], conv_rx.at[sixteen(s)], conv_s, conv_r, s)
    conv_rx[sixteen(s), :] = conv_t[sixteen(s), :]
    for r in range(0, ROWS, WIDE):
        rows = pl.ds(r, WIDE)
        grad_outer[rows, :] = (acc[rows, :] * conv_output[rows, :].astype(F32)).astype(BF16)
    ring.end()
    edge.wait_send()
    left(taps, taps_s, taps_r, s)
    left(mix_t.at[sixteen(0)], mix_s, mix_r, s)
    arrived(lambda d: mix_rx.at[sixteen(d)], mix_s, mix_r, s)
    left(conv_t.at[sixteen(0)], conv_s, conv_r, s)
    arrived(lambda d: conv_rx.at[sixteen(d)], conv_s, conv_r, s)


def halves(x):
    high = x.astype(BF16)
    return high, (x - high.astype(F32)).astype(BF16)


def dot(a, b):
    return jnp.dot(a, b, preferred_element_type=F32)


def dot_three(x, table_h, table_l):
    high, low = halves(x)
    return dot(high, table_h) + dot(high, table_l) + dot(low, table_h)


def middle_kernel(
    in_shard, upstream, product_t, conv_cols, mix_cols, filters,
    first, second_h, second_l, third_h, third_l, last, cos_t, sin_t,
    grad_mixed, grad_long, grad_outproj, whole,
    conv_f, mix_f, out_f,
    gather_0, gather_1, gather_2, gather_3, gather_4,
    *scatter,
):
    at = place()
    s, y, z, c = at
    barrier = pltpu.get_barrier_semaphore()
    for there in (
        at_seq(y, (z + 1) % 8, c),
        at_seq(y, (z + 7) % 8, c),
        at_seq(1 - y, z, c),
        at_seq(y, z, 1 - c),
    ):
        pl.semaphore_signal(barrier, inc=1, device_id={"seq": there}, device_id_type=MESH)
    pl.semaphore_wait(barrier, 4)

    ring = Gather(in_shard, whole, (gather_0, gather_1, gather_2, gather_3, gather_4), at)
    total = Scatter(scatter, at)
    ring.begin()
    total.partials(product_t, upstream)
    gather_step = ring.steps()
    scatter_step = total.steps()
    for q in range(3):
        conv_f[q] = conv_cols[:, q * WIDE : (q + 1) * WIDE].astype(F32)
        mix_f[q] = mix_cols[:, q * WIDE : (q + 1) * WIDE].astype(F32)

    def channel(i, _):
        def read(ref):
            return jnp.concatenate(
                [ref[q, pl.ds(i, N_SEQ, stride=MINE), :] for q in range(3)], axis=0
            ).astype(BF16)

        signals = jnp.concatenate([read(conv_f), filters[i], read(mix_f)], axis=1)
        both = dot(first[...], signals)
        both = both[: 2 * OUTER] + both[2 * OUTER :]
        cos, sin = cos_t[...], sin_t[...]
        rows = []
        for n in range(3):
            re = both[:OUTER, n * WIDE : (n + 1) * WIDE]
            im = both[OUTER:, n * WIDE : (n + 1) * WIDE]
            rows.append(jnp.concatenate([re * cos + im * sin, im * cos - re * sin], axis=1))
        spec = dot_three(jnp.concatenate(rows, axis=0), second_h[...], second_l[...])
        g_re, g_im = spec[:OUTER, :WIDE], spec[:OUTER, WIDE:]
        rows = []
        for n in (1, 2):
            re = spec[n * OUTER : (n + 1) * OUTER, :WIDE]
            im = spec[n * OUTER : (n + 1) * OUTER, WIDE:]
            rows.append(jnp.concatenate([g_re * re + g_im * im, g_im * re - g_re * im], axis=1))
        mid = dot_three(jnp.concatenate(rows, axis=0), third_h[...], third_l[...])
        for n in range(2):
            re = mid[n * OUTER : (n + 1) * OUTER, :WIDE]
            im = mid[n * OUTER : (n + 1) * OUTER, WIDE:]
            turned = jnp.concatenate([re * cos - im * sin, im * cos + re * sin], axis=0)
            high, low = halves(turned)
            result = dot(last[2 * n], high) + dot(last[2 * n + 1], high) + dot(last[2 * n], low)
            if n == 0:
                for q in range(3):
                    out_f[q, pl.ds(i, N_SEQ, stride=MINE), :] = result[
                        q * N_SEQ : (q + 1) * N_SEQ
                    ]
            else:
                grad_long[i] = result
        return 0

    for n in range(8):
        next(gather_step, None)
        next(scatter_step, None)
        lax.fori_loop(2 * n, 2 * n + 2, channel, 0)
    for q in range(3):
        grad_mixed[:, q * WIDE : (q + 1) * WIDE] = out_f[q].astype(BF16)
    for _ in range(16):
        next(gather_step, None)
        next(scatter_step, None)
    total.finish(grad_outproj)
    for sub in range(2):
        for o in range(-3, 5):
            ring.ready(sub, o)
    ring.end()


def back_kernel(
    mixed_cols, padded, all_taps, gate, layer_input, weights,
    grad_inner, grad_input, grad_inproj, grad_short,
    mixed_rx, grads, halo, value, value_t, blocks, short_tx, short_rx, acc,
    halo_sem, mix_s, mix_r, short_s, short_r, x_s, x_r, p_s,
    *scatter,
):
    at = place()
    s, y, z, c = at
    ch = lax.axis_index("ch")
    x, low = ch % 4, ch // 4
    barrier = pltpu.get_barrier_semaphore()
    greet_all(barrier, s)
    for there in (low * 4 + (x + 1) % 4, low * 4 + (x + 3) % 4, (1 - low) * 4 + x):
        pl.semaphore_signal(barrier, inc=1, device_id={"ch": there}, device_id_type=MESH)
    pl.semaphore_wait(barrier, N_SEQ - 1 + 3)

    exchange(lambda d: mixed_cols.at[sixteen(d)], mixed_rx.at[sixteen(s)], mix_s, mix_r, s)
    mixed_rx[sixteen(s), :] = mixed_cols[sixteen(s), :]
    arrived(lambda d: mixed_rx.at[sixteen(d)], mix_s, mix_r, s)

    edge = remote(
        grads.at[pl.ds(0, 8)],
        halo,
        halo_sem.at[0],
        halo_sem.at[1],
        "seq",
        (s + N_SEQ - 1) % N_SEQ,
    )
    for r in range(0, ROWS, WIDE):
        rows = pl.ds(r, WIDE)
        mixed = mixed_rx[:, rows].astype(F32).T
        grads[rows, :] = mixed * gate[rows, :].astype(F32)
        if r == 0:
            edge.start()
        smooth = all_taps[pl.ds(0, 1), :] * padded[pl.ds(8 + r, WIDE), :]
        for j in range(1, 3):
            smooth = smooth + all_taps[pl.ds(j, 1), :] * padded[pl.ds(8 + r - j, WIDE), :]
        grad_inner[rows, :] = (mixed * smooth).astype(BF16)
    edge.wait_recv()
    grads[pl.ds(ROWS, 8), :] = jnp.where(s == N_SEQ - 1, 0.0, halo[...])
    for r in range(0, ROWS, WIDE):
        rows = pl.ds(r, WIDE)
        out = all_taps[pl.ds(0, 1), :] * grads[rows, :]
        for j in range(1, 3):
            out = out + all_taps[pl.ds(j, 1), :] * grads[pl.ds(r + j, WIDE), :]
        value[rows, :] = out.astype(BF16)
        value_t[:, rows] = out.T.astype(BF16)

    def block(sub, o):
        return (1 - low if sub else low) * 4 + (x + o + 4) % 4

    def x_source(sub, o):
        return value if (sub, o) == (0, 0) else blocks.at[block(sub, o)]

    def x_hop(di, d, sub):
        o = -SIGNS[di] * (d - 1)
        return remote(
            x_source(sub, o),
            blocks.at[block(sub, o)],
            x_s.at[di, d - 1, sub],
            x_r.at[di, d - 1, sub],
            "ch",
            low * 4 + (x + SIGNS[di] + 4) % 4,
        )

    def x_wait(di, d, sub):
        here = blocks.at[block(sub, -SIGNS[di] * d)]
        remote(
            here, here, x_s.at[di, d - 1, sub], x_r.at[di, d - 1, sub], "ch", ch
        ).wait_recv()

    partner = remote(
        value, blocks.at[block(0, 0)], p_s.at[0], p_s.at[1], "ch", (1 - low) * 4 + x
    )
    hops = [x_hop(0, 1, 0), x_hop(1, 1, 0)]
    hops[0].start()
    hops[1].start()
    partner.start()
    blocks[block(0, 0)] = value[...]

    total = Scatter(scatter, at)
    total.partials(value_t, layer_input)
    step = total.steps()
    next(step)
    next(step)

    sums = []
    for j in range(3):
        part = jnp.zeros((1, CHANS), F32)
        for r in range(0, ROWS, WIDE):
            part = part + jnp.sum(
                grads[pl.ds(r, WIDE), :] * padded[pl.ds(8 + r - j, WIDE), :], axis=0, keepdims=True
            )
        sums.append(part)
    short_tx[...] = jnp.concatenate(sums + [jnp.zeros((5, CHANS), F32)], axis=0)

    def lanes(d):
        return short_tx.at[:, pl.ds(pl.multiple_of(d // 8 * WIDE, WIDE), WIDE)]

    exchange(lanes, short_rx.at[s], short_s, short_r, s)
    short_rx[s] = short_tx[:, pl.ds(pl.multiple_of(s // 8 * WIDE, WIDE), WIDE)]

    def multiply(n, first=False):
        w = jnp.concatenate([weights[4 * n + i] for i in range(4)], axis=0)
        part = lax.dot_general(
            blocks[n], w, (((1,), (1,)), ((), ())), preferred_element_type=F32
        )
        acc[...] = part if first else acc[...] + part

    multiply(ch, True)
    next(step)
    partner.wait_recv()
    for di in range(2):
        hop = x_hop(di, 1, 1)
        hop.start()
        hops.append(hop)
    multiply(block(1, 0))
    next(step)
    x_wait(0, 1, 0)
    hop = x_hop(0, 2, 0)
    hop.start()
    hops.append(hop)
    multiply(block(0, -1))
    next(step)
    x_wait(1, 1, 0)
    multiply(block(0, 1))
    next(step)
    x_wait(1, 1, 1)
    hop = x_hop(1, 2, 1)
    hop.start()
    hops.append(hop)
    multiply(block(1, 1))
    for _ in step:
        pass
    x_wait(0, 1, 1)
    multiply(block(1, -1))
    total.finish(grad_inproj)
    arrived(lambda d: short_rx.at[d], short_s, short_r, s)
    tile = short_rx[0]
    for i in range(1, N_SEQ):
        tile = tile + short_rx[i]
    grad_short[...] = tile
    x_wait(0, 2, 0)
    multiply(block(0, 2))
    x_wait(1, 2, 1)
    multiply(block(1, 2))
    grad_input[...] = acc[...].astype(BF16)
    for hop in hops:
        hop.wait_send()
    partner.wait_send()
    edge.wait_send()
    left(mixed_cols.at[sixteen(0)], mix_s, mix_r, s)
    left(short_rx.at[0], short_s, short_r, s)


def call(kernel, outs, scratch, collective_id, args, flops):
    vmem = pl.BlockSpec(memory_space=pltpu.VMEM)
    return pl.pallas_call(
        kernel,
        out_shape=[jax.ShapeDtypeStruct(shape, dtype) for shape, dtype in outs],
        in_specs=[vmem] * len(args),
        out_specs=[vmem] * len(outs),
        scratch_shapes=scratch,
        compiler_params=pltpu.CompilerParams(
            collective_id=collective_id, has_side_effects=True, vmem_limit_bytes=50 * 2**20
        ),
        cost_estimate=pl.CostEstimate(
            flops=flops, bytes_accessed=20 * 2**20, transcendentals=0
        ),
    )(*args)


def shards(
    layer_input, value_proj, outer_gate, inner_gate, conv_output,
    upstream, in_weight, out_weight, long_filter, short_filter,
):
    s = lax.axis_index("seq")
    dma = pltpu.SemaphoreType.DMA
    peers = dma((N_SEQ,))
    turned = [
        ((4 * to + i) * 8 + ch, (4 * ch + i) * 8 + to)
        for to in range(8)
        for ch in range(8)
        for i in range(4)
    ]
    in_piece = lax.ppermute(in_weight, ("seq", "ch"), turned)
    lane = (s % 8) * MINE
    taps = lax.dynamic_update_slice(
        jnp.zeros((8, WIDE), F32), short_filter[0].T, (jnp.int32(0), lane.astype(jnp.int32))
    )
    filters = long_filter[0].reshape(MINE, N_SEQ, 3, WIDE)
    filters = filters.transpose(0, 2, 1, 3).reshape(MINE, OUTER, WIDE)

    grad_outer, product_t, conv_cols, mix_cols, padded, all_taps = call(
        front_kernel,
        [
            ((ROWS, CHANS), BF16),
            ((CHANS, ROWS), BF16),
            ((CHANS, ROWS), BF16),
            ((CHANS, ROWS), BF16),
            ((ROWS + 8, CHANS), F32),
            ((8, CHANS), F32),
        ],
        [
            pltpu.VMEM((N_SEQ, CHANS, WIDE), BF16),
            pltpu.VMEM((ROWS, CHANS), F32),
            pltpu.VMEM((CHANS, ROWS), BF16),
            pltpu.VMEM((CHANS, ROWS), BF16),
            pltpu.VMEM((16, CHANS), BF16),
            pltpu.VMEM((N_SEQ, 8, WIDE), F32),
            *Gather.sems,
            dma((2,)), peers, peers, peers, peers, peers, peers,
        ],
        0,
        (out_weight, upstream, outer_gate, conv_output, value_proj, inner_gate, taps),
        2 * 10**9,
    )
    tables = [jnp.asarray(t) for t in dft_tables()]
    grad_mixed, grad_long, grad_outproj, weights = call(
        middle_kernel,
        [
            ((CHANS, ROWS), BF16),
            ((MINE, OUTER, WIDE), F32),
            ((CHANS, WIDE), F32),
            ((N_SEQ, WIDE, CHANS), BF16),
        ],
        [
            pltpu.VMEM((3, CHANS, WIDE), F32),
            pltpu.VMEM((3, CHANS, WIDE), F32),
            pltpu.VMEM((3, CHANS, WIDE), F32),
            *Gather.sems,
            *Scatter.scratch(),
        ],
        1,
        (in_piece, upstream, product_t, conv_cols, mix_cols, filters, *tables),
        6 * 10**9,
    )
    grad_inner, grad_input, grad_inproj, grad_short = call(
        back_kernel,
        [
            ((ROWS, CHANS), BF16),
            ((ROWS, CHANS), BF16),
            ((CHANS, WIDE), F32),
            ((8, WIDE), F32),
        ],
        [
            pltpu.VMEM((CHANS, ROWS), BF16),
            pltpu.VMEM((ROWS + 8, CHANS), F32),
            pltpu.VMEM((8, CHANS), F32),
            pltpu.VMEM((ROWS, CHANS), BF16),
            pltpu.VMEM((CHANS, ROWS), BF16),
            pltpu.VMEM((8, ROWS, CHANS), BF16),
            pltpu.VMEM((8, CHANS), F32),
            pltpu.VMEM((N_SEQ, 8, WIDE), F32),
            pltpu.VMEM((ROWS, CHANS), F32),
            dma((2,)), peers, peers, peers, peers, dma((2, 2, 2)), dma((2, 2, 2)), dma((2,)),
            *Scatter.scratch(),
        ],
        2,
        (grad_mixed, padded, all_taps, inner_gate, layer_input, weights),
        4 * 10**9,
    )
    grad_taps = lax.dynamic_slice(
        grad_short, (jnp.int32(0), lane.astype(jnp.int32)), (3, MINE)
    ).T
    return (
        grad_input,
        grad_outer,
        grad_inner,
        grad_long.reshape(1, MINE, LENGTH),
        grad_taps[None],
        grad_inproj.T,
        grad_outproj,
    )


def solution(mesh):
    in_specs = (
        P("seq", None),
        P("seq", "ch"),
        P("seq", "ch"),
        P("seq", "ch"),
        P("seq", "ch"),
        P("seq", None),
        P("seq", "ch"),
        P("ch", "seq"),
        P("ch", "seq", None),
        P("ch", "seq", None),
    )
    out_specs = (
        P("seq", "ch"),
        P("seq", "ch"),
        P("seq", "ch"),
        P("ch", "seq", None),
        P("ch", "seq", None),
        P("seq", "ch"),
        P("ch", "seq"),
    )
    return jax.shard_map(shards, mesh=mesh, in_specs=in_specs, out_specs=out_specs, check_vma=False)
```

time: 551 us -> 205 us (0.37); the launches traced: 540 us -> 202 us
  waiting for transfers between devices: 376 us -> 0.01 us
  Pallas kernels: 0 us -> 180 us
  matrix products: 45.9 us -> 0 us
  starting transfers between devices: 31.1 us -> 8.86 us
  blocking collectives: 21.6 us -> 0 us
  other arithmetic: 20.9 us -> 0 us
  local copies, waits for them, and re-layouts: 29.6 us -> 13.2 us
  between operations: 14.4 us -> 0.85 us
    unnamed x7 -> x0, waiting for transfers between devices: 231 us -> none
    pallas_call x0 -> x3, Pallas kernels: none -> 180 us  [call(): pl.pallas_call(kernel, out_shape=[jax.ShapeDtypeStruct(shape, dtype) for...]
    reduce_scatter x1 -> x0, waiting for transfers between devices: 76.4 us -> none  [shards(): lax.psum_scatter(partial_input, 'ch', scatter_dimension=1, tiled=True)]
    dot_general x8 -> x0, matrix products: 45.9 us -> none  [the longest x1 10.6 us: forward_dft(): jnp.einsum('ckb,bm->ckm', joined, forward_inner, precision=lax.Precision....]
    all_gather x2 -> x0, waiting for transfers between devices: 41.6 us -> none  [the longest x1 41.6 us: shards(): lax.all_gather(out_weight, 'seq', axis=1, tiled=True)]
    all_to_all x4 -> x0, starting transfers between devices: 30.4 us -> none  [the longest x1 11 us: shards(): lax.all_to_all(value_proj, 'seq', split_axis=1, concat_axis=0, tiled=True)]
    all_to_all x4 -> x0, waiting for transfers between devices: 27.6 us -> none  [the longest x1 14.7 us: shards(): lax.all_to_all(grad_conv, 'seq', split_axis=1, concat_axis=0, tiled=True)]
    all_to_all x1 -> x0, blocking collectives: 21.6 us -> none  [shards(): lax.all_to_all(grad_value_cols.T, 'seq', split_axis=0, concat_axis=1, til...]
  transfers between devices with their start and end apart: 9 -> 1, of which waited for: 7 -> 0; matrix products, arithmetic and copies ran while one was open for 17% -> 1% of each run, Pallas kernels for 0% -> 29%
where the time goes in v1:
time: 205 us; the launch traced here: 202 us
  Pallas kernels  180 us (88%)
  local copies, waits for them, and re-layouts  13.2 us (6%)
  starting transfers between devices  8.86 us (4%)
    pallas_call x3, Pallas kernels, call(): pl.pallas_call(kernel, out_shape=[jax.ShapeDtypeStruct(shape, dtype) for...  180 us
    unnamed x35, local copies, waits for them, and re-layouts  9.96 us
    ppermute x1, starting transfers between devices, shards(): in_piece = lax.ppermute(in_weight, ('seq', 'ch'), turned)  8.86 us
  transfers between devices with their start and end apart: 1, of which 0 were waited for; matrix products, arithmetic and copies ran while one was open for 1% of the time, Pallas kernels for 29%

profile of v1, /device:TPU:15, one launch (start us, length us, event | category | flops | bytes accessed | tf_op | source)
XLA Modules:
  0.0 202.4 jit_solution(11868534470547044616)
XLA Ops:
  0.6 8.9 %collective-permute-start = (bf16[128,512]{1,0:T(8,128)(2,1)}, bf16[128,512]{1,0:T(8,128)(2,1)S(1)}, u32[]{:S(2)}, u32[]{:S(2)}) collective-permute-start(bf16[128,512]{1,0:T(8,128)(2,1)} %param.24), channel_id=1, source_target_pairs={{0,0},{8,8},{16,16},{24,24},{1,32},{9,40},{17,48},{25,56},{2,64},{... | collective-permute-start | bytes 393224 | tf_op jit(solution)/shard_map/ppermute | solution.py:745
  9.5 0.7 copy.33
  10.2 1.6 reshape_squeeze.3
  11.8 0.1 copy.28
  11.8 0.5 dynamic_update_slice.3.taps
  12.3 0.0 copy-start
  12.4 1.0 copy-done
  13.3 0.0 copy-start.1
  13.3 1.0 copy-done.1
  14.3 0.0 copy-start.2
  14.3 1.0 copy-done.2
  15.3 0.0 copy-start.3
  15.3 1.0 copy-done.3
  16.3 0.0 copy-start.5
  16.3 0.9 copy-done.5
  17.2 0.0 copy-start.6
  17.2 0.0 copy-start.7
  17.2 0.0 copy-start.8
  17.2 0.0 copy-start.9
  17.3 0.0 copy-start.10
  17.3 0.0 copy-start.11
  17.3 0.0 copy-start.12
  17.3 0.0 copy-start.13
  17.3 58.9 %shard_map.225 = (bf16[384,512]{1,0:T(8,128)(2,1)S(1)}, bf16[512,384]{1,0:T(8,128)(2,1)S(1)}, bf16[512,384]{1,0:T(8,128)(2,1)S(1)}, bf16[512,384]{1,0:T(8,128)(2...) custom-call(bf16[512,128]{1,0:T(8,128)(2,1)S(1)} %copy-done.5, bf16[384,4096]{1,0:T(8,128)(2,1)} %upstream.3, ...), custom_call_target="tpu_custom_call" | custom-call | flops 2000000000 | bytes 20971520 | tf_op jit(solution)/shard_map/pallas_call | solution.py:717
  76.2 0.0 collective-permute-done.in_shard
  76.2 0.0 copy-done.6
  76.2 0.0 copy-done.7
  76.2 0.0 copy-done.8
  76.2 0.0 copy-done.9
  76.2 0.0 copy-done.10
  76.3 0.0 copy-done.11
  76.3 0.0 copy-done.12
  76.3 0.0 copy-done.13
  76.3 0.0 copy-start.4
  76.3 57.7 %shard_map.226 = (bf16[512,384]{1,0:T(8,128)(2,1)S(1)}, f32[16,96,128]{2,1,0:T(8,128)S(1)}, f32[512,128]{1,0:T(8,128)S(1)}, bf16[32,128,512]{2,1,0:T(8,128)(2,1)}) custom-call(bf16[128,512]{1,0:T(8,128)(2,1)S(1)} %collective-permute-done.in_shard, bf16[384,4096]{1,0:T(8,128)(2,1)} %upstream.3, bf16[512,384]{1,0:T(8,128)(2,1)S(1)} %get-tuple-element.21.product_t, ...), custom_call_target="tpu_custom_call" | custom-call | flops 6000000000 | bytes 20971520 | tf_op jit(solution)/shard_map/pallas_call | solution.py:717
  134.0 0.0 copy-done.4
  134.0 62.9 %shard_map.227 = (bf16[384,512]{1,0:T(8,128)(2,1)S(1)}, bf16[384,512]{1,0:T(8,128)(2,1)S(1)}, f32[512,128]{1,0:T(8,128)S(1)}, f32[8,128]{1,0:T(8,128)S(1)}) custom-call(bf16[512,384]{1,0:T(8,128)(2,1)S(1)} %get-tuple-element.24.mixed_cols, f32[392,512]{1,0:T(8,128)S(1)} %get-tuple-element.25.padded, f32[8,512]{1,0:T(8,128)S(1)} %get-tuple-element.26.all_taps, ...), custom_call_target="tpu_custom_call" | custom-call | flops 4000000000 | bytes 20971520 | tf_op jit(solution)/shard_map/pallas_call | solution.py:717
  196.9 0.1 dynamic-slice_bitcast_fusion
  197.0 0.6 copy.29
  197.6 0.8 copy.30
  198.4 1.0 reshape.21
  199.4 0.7 copy.39
  200.2 0.7 copy.40
  200.9 0.7 copy.41
  201.7 0.7 copy.42
  (1 shorter events, 0.0 us)
Async XLA Ops:
  0.6 75.6 %collective-permute-start = (bf16[128,512]{1,0:T(8,128)(2,1)}, bf16[128,512]{1,0:T(8,128)(2,1)S(1)}, u32[]{:S(2)}, u32[]{:S(2)}) collective-permute-start(bf16[128,512]{1,0:T(8,128)(2,1)} %param.24), channel_id=1, source_target_pairs={{0,0},{8,8},{16,16},{24,24},{1,32},{9,40},{17,48},{25,56},{2,64},{... | collective-permute-start | bytes 393224 | tf_op jit(solution)/shard_map/ppermute | solution.py:745
  12.3 1.0 copy-start
  13.3 1.0 copy-start.1
  14.3 1.0 copy-start.2
  15.3 1.0 copy-start.3
  16.3 0.9 copy-start.5
  17.2 59.0 %copy-start.6 = (bf16[4,96,192]{2,1,0:T(8,128)(2,1)S(1)}, bf16[4,96,192]{2,1,0:T(8,128)(2,1)}, u32[]{:S(2)}) copy-start(bf16[4,96,192]{2,1,0:T(8,128)(2,1)} %constant.47.clone.last) | copy-start | bytes 442372
  17.2 59.0 %copy-start.7 = (bf16[256,256]{1,0:T(8,128)(2,1)S(1)}, bf16[256,256]{1,0:T(8,128)(2,1)}, u32[]{:S(2)}) copy-start(bf16[256,256]{1,0:T(8,128)(2,1)} %constant.46.clone.third_l) | copy-start | bytes 393220
  17.2 59.0 %copy-start.8 = (bf16[256,256]{1,0:T(8,128)(2,1)S(1)}, bf16[256,256]{1,0:T(8,128)(2,1)}, u32[]{:S(2)}) copy-start(bf16[256,256]{1,0:T(8,128)(2,1)} %constant.45.clone.third_h) | copy-start | bytes 393220
  17.2 59.0 %copy-start.9 = (bf16[256,256]{1,0:T(8,128)(2,1)S(1)}, bf16[256,256]{1,0:T(8,128)(2,1)}, u32[]{:S(2)}) copy-start(bf16[256,256]{1,0:T(8,128)(2,1)} %constant.44.clone.second_l) | copy-start | bytes 393220
  17.3 59.0 %copy-start.10 = (bf16[256,256]{1,0:T(8,128)(2,1)S(1)}, bf16[256,256]{1,0:T(8,128)(2,1)}, u32[]{:S(2)}) copy-start(bf16[256,256]{1,0:T(8,128)(2,1)} %constant.43.clone.second_h) | copy-start | bytes 393220
  17.3 59.0 %copy-start.11 = (bf16[384,96]{1,0:T(8,128)(2,1)S(1)}, bf16[384,96]{1,0:T(8,128)(2,1)}, u32[]{:S(2)}) copy-start(bf16[384,96]{1,0:T(8,128)(2,1)} %constant.42.clone.first) | copy-start | bytes 221188
  17.3 59.0 %copy-start.12 = (f32[96,128]{1,0:T(8,128)S(1)}, f32[96,128]{1,0:T(8,128)}, u32[]{:S(2)}) copy-start(f32[96,128]{1,0:T(8,128)} %constant.49.clone.sin_t) | copy-start | bytes 147460
  17.3 59.0 %copy-start.13 = (f32[96,128]{1,0:T(8,128)S(1)}, f32[96,128]{1,0:T(8,128)}, u32[]{:S(2)}) copy-start(f32[96,128]{1,0:T(8,128)} %constant.48.clone.cos_t) | copy-start | bytes 147460
  76.3 57.7 %copy-start.4 = (bf16[384,512]{1,0:T(8,128)(2,1)S(1)}, bf16[384,512]{1,0:T(8,128)(2,1)}, u32[]{:S(2)}) copy-start(bf16[384,512]{1,0:T(8,128)(2,1)} %gate.3) | copy-start | bytes 1179652

commit v2 on v1

v2 whole, which is shorter than its diff:
```python
import math

import ml_dtypes
import numpy as np
import jax
import jax.numpy as jnp
from jax import lax
from jax.experimental import pallas as pl
from jax.experimental.pallas import tpu as pltpu
from jax.sharding import PartitionSpec as P

MESH = pl.DeviceIdType.MESH
F32 = jnp.float32
BF16 = jnp.bfloat16
N_SEQ = 32
ROWS = 384
CHANS = 512
MINE = 16
WIDE = 128
DEEP = 4096
LENGTH = N_SEQ * ROWS
OUTER = LENGTH // WIDE
SIGNS = (1, -1)


def split_table(table):
    high = table.astype(ml_dtypes.bfloat16)
    low = (table - high.astype(np.float64)).astype(ml_dtypes.bfloat16)
    return high, low


def dft_tables():
    a = np.arange(OUTER)
    b = np.arange(WIDE)
    k1 = np.arange(OUTER)
    k2 = np.arange(WIDE)
    turn = np.pi / (2 * LENGTH)
    outer = 2 * np.pi * np.outer(k1, a) / OUTER + turn * WIDE * a[None, :]
    twist = 2 * np.pi * np.outer(k1, b) / LENGTH + turn * b[None, :]
    inner = 2 * np.pi * np.outer(b, k2) / WIDE
    first = np.concatenate([np.cos(outer), -np.sin(outer)], axis=0)
    co, si = np.cos(inner), np.sin(inner)
    second = np.block([[co, -si], [si, co]])
    third = np.block([[co, si], [-si, co]])
    last = np.concatenate([np.cos(outer).T, -np.sin(outer).T], axis=1) / LENGTH
    first_h, first_l = split_table(first)
    second_h, second_l = split_table(second)
    third_h, third_l = split_table(third)
    last_h, last_l = split_table(last)
    return (
        np.concatenate([first_h, first_l], axis=0),
        second_h,
        second_l,
        third_h,
        third_l,
        np.stack([last_h, last_l]),
        np.cos(twist).astype(np.float32),
        np.sin(twist).astype(np.float32),
    )


def remote_to(src, dst, send, recv, device):
    return pltpu.make_async_remote_copy(
        src_ref=src,
        dst_ref=dst,
        send_sem=send,
        recv_sem=recv,
        device_id=device,
        device_id_type=MESH,
    )


def remote(src, dst, send, recv, axis, index):
    return remote_to(src, dst, send, recv, {axis: index})


def place():
    s = lax.axis_index("seq")
    return s, s // 16, (s // 2) % 8, s % 2


def at_seq(y, z, c):
    return y * 16 + z * 2 + c


def greet_all(barrier, s):
    def body(i, _):
        pl.semaphore_signal(
            barrier, inc=1, device_id={"seq": (s + i) % N_SEQ}, device_id_type=MESH
        )
        return 0

    lax.fori_loop(1, N_SEQ, body, 0)


def exchange(source_of, target, sends, recvs, s):
    def body(i, _):
        dst = (s + i) % N_SEQ
        remote(source_of(dst), target, sends.at[i], recvs.at[i], "seq", dst).start()
        return 0

    lax.fori_loop(1, N_SEQ, body, 0)


def arrived(landing_of, sends, recvs, s):
    def body(i, _):
        src = (s + N_SEQ - i) % N_SEQ
        here = landing_of(src)
        remote(here, here, sends.at[i], recvs.at[i], "seq", src).wait_recv()
        return 0

    lax.fori_loop(1, N_SEQ, body, 0)


def left(piece, sends, recvs, s):
    def body(i, _):
        remote(piece, piece, sends.at[i], recvs.at[i], "seq", (s + i) % N_SEQ).wait_send()
        return 0

    lax.fori_loop(1, N_SEQ, body, 0)


class Gather:
    sems = [
        pltpu.SemaphoreType.DMA((2, 4, 2)),
        pltpu.SemaphoreType.DMA((2, 4, 2)),
        pltpu.SemaphoreType.DMA((2, 8)),
        pltpu.SemaphoreType.DMA((2, 8)),
        pltpu.SemaphoreType.DMA((3,)),
    ]

    def __init__(self, shard, whole, sems, at):
        self.shard, self.whole, self.at = shard, whole, at
        self.zs, self.zr, self.cs, self.cr, self.ys = sems
        self.started = []

    def slot(self, sub, o, other=False):
        _, y, z, c = self.at
        yy = 1 - y if sub else y
        return at_seq(yy, (z + o + 8) % 8, 1 - c if other else c)

    def go(self, copy):
        copy.start()
        self.started.append(copy)

    def source(self, sub, o):
        if sub == 0 and o == 0:
            return self.shard
        return self.whole.at[self.slot(sub, o)]

    def hop(self, di, d, sub):
        _, y, z, c = self.at
        o = -SIGNS[di] * (d - 1)
        there = at_seq(y, (z + SIGNS[di] + 8) % 8, c)
        self.go(
            remote(
                self.source(sub, o),
                self.whole.at[self.slot(sub, o)],
                self.zs.at[di, d - 1, sub],
                self.zr.at[di, d - 1, sub],
                "seq",
                there,
            )
        )

    def share(self, sub, o):
        _, y, z, c = self.at
        self.go(
            remote(
                self.source(sub, o),
                self.whole.at[self.slot(sub, o)],
                self.cs.at[sub, o % 8],
                self.cr.at[sub, o % 8],
                "seq",
                at_seq(y, z, 1 - c),
            )
        )

    def pair(self):
        _, y, z, c = self.at
        return remote(
            self.shard,
            self.whole.at[self.slot(0, 0)],
            self.ys.at[0],
            self.ys.at[1],
            "seq",
            at_seq(1 - y, z, c),
        )

    @staticmethod
    def travels(di, d, sub):
        return d < 4 or (d == 4 and sub == di)

    def begin(self):
        self.hop(0, 1, 0)
        self.hop(1, 1, 0)
        self.go(self.pair())
        self.share(0, 0)
        self.keep = pltpu.make_async_copy(
            self.shard, self.whole.at[self.slot(0, 0)], self.ys.at[2]
        )
        self.keep.start()

    def steps(self):
        self.pair().wait_recv()
        self.hop(0, 1, 1)
        self.hop(1, 1, 1)
        self.share(1, 0)
        yield
        for d in range(1, 5):
            for sub in range(2):
                for di in range(2):
                    if not self.travels(di, d, sub):
                        continue
                    o = -SIGNS[di] * d
                    here = self.whole.at[self.slot(sub, o)]
                    remote(
                        here,
                        here,
                        self.zs.at[di, d - 1, sub],
                        self.zr.at[di, d - 1, sub],
                        "seq",
                        self.at[0],
                    ).wait_recv()
                    if self.travels(di, d + 1, sub):
                        self.hop(di, d + 1, sub)
                    self.share(sub, o)
                yield

    def ready(self, sub, o):
        _, y, z, c = self.at
        if (sub, o) == (0, 0):
            self.keep.wait()
        here = self.whole.at[self.slot(sub, o, other=True)]
        remote(
            here, here, self.cs.at[sub, o % 8], self.cr.at[sub, o % 8], "seq", self.at[0]
        ).wait_recv()
        yy = 1 - y if sub else y
        return yy * 8 + (z + o + 8) % 8

    def end(self):
        for copy in self.started:
            copy.wait_send()


class Scatter:
    @staticmethod
    def scratch():
        return [
            pltpu.VMEM((2, 8, CHANS, WIDE), BF16),
            pltpu.VMEM((2, 8, CHANS, WIDE), BF16),
            pltpu.VMEM((2, 8, CHANS, WIDE), BF16),
            pltpu.VMEM((2, 4, 2, CHANS, WIDE), BF16),
            pltpu.VMEM((2, CHANS, WIDE), BF16),
            pltpu.SemaphoreType.DMA((2, 4, 2)),
            pltpu.SemaphoreType.DMA((2, 4, 2)),
            pltpu.SemaphoreType.DMA((2, 8)),
            pltpu.SemaphoreType.DMA((2, 8)),
            pltpu.SemaphoreType.DMA((2,)),
        ]

    def __init__(self, scratch, at):
        self.at = at
        self.own, self.tx, self.rx, self.zrx, self.yrx = scratch[:5]
        self.zs, self.zr, self.cs, self.cr, self.ys = scratch[5:]
        self.started = []

    def go(self, copy):
        copy.start()
        self.started.append(copy)

    def hand(self, sub, o):
        _, y, z, c = self.at
        return remote(
            self.tx.at[sub, o],
            self.rx.at[sub, o],
            self.cs.at[sub, o],
            self.cr.at[sub, o],
            "seq",
            at_seq(y, z, 1 - c),
        )

    def partials(self, left_t, right, first=0, last=8):
        _, y, z, c = self.at

        def body(i, _):
            o = (4 + (1 - 2 * (i % 2)) * ((i + 1) // 2) + 8) % 8
            columns = []
            for sub in range(2):
                m = (1 - y if sub else y) * 8 + (z + o) % 8
                columns.append(right[:, pl.ds(pl.multiple_of(m * 2 * WIDE, 2 * WIDE), 2 * WIDE)])
            both = jnp.dot(
                left_t[...], jnp.concatenate(columns, axis=1), preferred_element_type=F32
            )
            for sub in range(2):
                low = both[:, 2 * sub * WIDE : (2 * sub + 1) * WIDE].astype(BF16)
                high = both[:, (2 * sub + 1) * WIDE : (2 * sub + 2) * WIDE].astype(BF16)
                self.tx[sub, o] = jnp.where(c == 0, high, low)
                self.hand(sub, o).start()
                self.own[sub, o] = jnp.where(c == 0, low, high)
            return 0

        lax.fori_loop(first, last, body, 0)

    def hop(self, di, d, sub):
        _, y, z, c = self.at
        o = (SIGNS[di] * d) % 8
        there = at_seq(y, (z + SIGNS[di] + 8) % 8, c)
        return remote(
            self.own.at[sub, o],
            self.zrx.at[di, d - 1, sub],
            self.zs.at[di, d - 1, sub],
            self.zr.at[di, d - 1, sub],
            "seq",
            there,
        )

    def pair(self):
        _, y, z, c = self.at
        return remote(
            self.yrx.at[0],
            self.yrx.at[1],
            self.ys.at[0],
            self.ys.at[1],
            "seq",
            at_seq(1 - y, z, c),
        )

    def both(self, sub, o):
        self.hand(sub, o).wait_recv()
        return self.own[sub, o].astype(F32) + self.rx[sub, o].astype(F32)

    def steps(self):
        for d in range(4, 0, -1):
            for sub in range(2):
                for di in range(2):
                    if not Gather.travels(di, d, sub):
                        continue
                    o = (SIGNS[di] * d) % 8
                    total = self.both(sub, o)
                    if Gather.travels(di, d + 1, sub):
                        self.hop(di, d + 1, sub).wait_recv()
                        total = total + self.zrx[di, d, sub].astype(F32)
                    self.own[sub, o] = total.astype(BF16)
                    self.go(self.hop(di, d, sub))
                yield

    def finish(self, out):
        def total(sub):
            value = self.both(sub, 0)
            for di in range(2):
                self.hop(di, 1, sub).wait_recv()
                value = value + self.zrx[di, 0, sub].astype(F32)
            return value

        self.yrx[0] = total(1).astype(BF16)
        self.pair().start()
        out[...] = total(0)
        self.pair().wait_recv()
        out[...] += self.yrx[1].astype(F32)
        self.pair().wait_send()
        for copy in self.started:
            copy.wait_send()

        def body(i, _):
            for sub in range(2):
                self.hand(sub, i).wait_send()
            return 0

        lax.fori_loop(0, 8, body, 0)


def sixteen(index):
    return pl.ds(pl.multiple_of(index * MINE, MINE), MINE)


def halves(x):
    high = x.astype(BF16)
    return high, (x - high.astype(F32)).astype(BF16)


def dot(a, b):
    return jnp.dot(a, b, preferred_element_type=F32)


def dot_three(x, table_h, table_l):
    high, low = halves(x)
    return dot(high, table_h[...]) + dot(high, table_l[...]) + dot(low, table_h[...])


class Spectra:
    def __init__(self, tables):
        (
            self.first,
            self.second_h,
            self.second_l,
            self.third_h,
            self.third_l,
            self.last,
            self.cos_t,
            self.sin_t,
        ) = tables

    def forward(self, source, i):
        signals = jnp.concatenate(
            [source[pl.ds(2 * i + n, OUTER, stride=MINE), :] for n in range(2)], axis=1
        ).astype(BF16)
        both = dot(self.first[...], signals)
        both = both[: 2 * OUTER] + both[2 * OUTER :]
        cos, sin = self.cos_t[...], self.sin_t[...]
        rows = []
        for n in range(2):
            re = both[:OUTER, n * WIDE : (n + 1) * WIDE]
            im = both[OUTER:, n * WIDE : (n + 1) * WIDE]
            rows.append(jnp.concatenate([re * cos + im * sin, im * cos - re * sin], axis=1))
        return dot_three(jnp.concatenate(rows, axis=0), self.second_h, self.second_l)

    def inverse(self, later, earlier, target, i):
        a, b = later[:, :WIDE], later[:, WIDE:]
        c, d = earlier[:, :WIDE], earlier[:, WIDE:]
        spec = jnp.concatenate([a * c + b * d, b * c - a * d], axis=1)
        mid = dot_three(spec, self.third_h, self.third_l)
        cos, sin = self.cos_t[...], self.sin_t[...]
        turned = []
        for n in range(2):
            re = mid[n * OUTER : (n + 1) * OUTER, :WIDE]
            im = mid[n * OUTER : (n + 1) * OUTER, WIDE:]
            turned.append(jnp.concatenate([re * cos - im * sin, im * cos + re * sin], axis=0))
        high, low = halves(jnp.concatenate(turned, axis=1))
        result = dot(self.last[0], high) + dot(self.last[1], high) + dot(self.last[0], low)
        for n in range(2):
            target[pl.ds(2 * i + n, OUTER, stride=MINE), :] = result[
                :, n * WIDE : (n + 1) * WIDE
            ]


def spread(cols, target):
    def body(s, _):
        for q in range(3):
            target[sixteen(3 * s + q), :] = cols[sixteen(s), q * WIDE : (q + 1) * WIDE].astype(F32)
        return 0

    lax.fori_loop(0, N_SEQ, body, 0)


def lanes_at(index):
    return pl.ds(pl.multiple_of(index * WIDE, WIDE), WIDE)


def whole_kernel(*refs):
    (
        layer_hbm, value_hbm, outer_hbm, gate_hbm, conv_hbm, up_hbm, in_shard, out_shard, filter_hbm, taps,
        *table_hbm,
    ) = refs[:18]
    (
        grad_input, grad_outer, grad_inner, grad_long, grad_short, grad_inproj, grad_outproj,
    ) = refs[18:25]
    (
        layer_input, value_in, outer_gate, gate, conv_output, upstream, filters, *tables,
    ) = refs[25:40]
    (
        whole_out, whole_in, acc, product_t, conv_t, mix_t, conv_rx, mix_rx, mixed_cols, mixed_rx,
        value, value_t, x_own, x_rx, y_io, padded, all_taps, halo, taps_rx, grads, halo_back, short_tx, short_rx,
        conv_f, other_f, out_f, spec_g, spec_h, inproj_t,
        load_sem, halo_sem, taps_s, taps_r, mix_s, mix_r, conv_s, conv_r,
        back_s, back_r, short_s, short_r, x_s, x_r, p_s,
    ) = refs[40:84]
    rest = refs[84:]
    sems_out, sems_in = rest[:5], rest[5:10]
    scatter_out, scatter_in = rest[10:20], rest[20:30]

    at = place()
    s, y, z, c = at
    ch = lax.axis_index("ch")
    x, low = ch % 4, ch // 4

    barrier = pltpu.get_barrier_semaphore()
    greet_all(barrier, s)
    for there in (low * 4 + (x + 1) % 4, low * 4 + (x + 3) % 4, (1 - low) * 4 + x):
        pl.semaphore_signal(barrier, inc=1, device_id={"ch": there}, device_id_type=MESH)

    sources = [outer_hbm, conv_hbm, value_hbm, gate_hbm, up_hbm, filter_hbm, layer_hbm, *table_hbm]
    targets = [outer_gate, conv_output, value_in, gate, upstream, filters, layer_input, *tables]
    loads = {}
    for n, (src, dst) in enumerate(zip(sources, targets)):
        copy = pltpu.make_async_copy(src, dst, load_sem.at[n])
        copy.start()
        loads[n] = copy

    def loaded(*which):
        for n in which:
            loads[n].wait()

    pl.semaphore_wait(barrier, N_SEQ - 1 + 3)

    ring = Gather(out_shard, whole_out, sems_out, at)
    ring.begin()
    edge = remote(
        value_hbm.at[pl.ds(ROWS - 16, 16)],
        halo,
        halo_sem.at[0],
        halo_sem.at[1],
        "seq",
        (s + 1) % N_SEQ,
    )
    edge.start()
    exchange(lambda d: taps, taps_rx.at[s], taps_s, taps_r, s)
    taps_own = pltpu.make_async_copy(taps, taps_rx.at[s], halo_sem.at[4])
    taps_own.start()
    step = ring.steps()
    loaded(0, 1)
    for r in range(0, ROWS, WIDE):
        rows = pl.ds(r, WIDE)
        product = outer_gate[rows, :].astype(F32) * conv_output[rows, :].astype(F32)
        product_t[:, rows] = product.T.astype(BF16)
    next(step)

    loaded(2, 3)
    for r in range(0, ROWS, WIDE):
        padded[pl.ds(8 + r, WIDE), :] = value_in[pl.ds(r, WIDE), :].astype(F32)
    arrived(lambda d: taps_rx.at[d], taps_s, taps_r, s)
    taps_own.wait()
    for g in range(4):
        tile = taps_rx[8 * g]
        for i in range(1, 8):
            tile = tile + taps_rx[8 * g + i]
        all_taps[:, pl.ds(g * WIDE, WIDE)] = tile
    edge.wait_recv()
    padded[pl.ds(0, 8), :] = jnp.where(s == 0, 0.0, halo[...].astype(F32)[8:, :])
    next(step)

    def smooth_rows(r):
        smooth = all_taps[pl.ds(0, 1), :] * padded[pl.ds(8 + r, WIDE), :]
        for j in range(1, 3):
            smooth = smooth + all_taps[pl.ds(j, 1), :] * padded[pl.ds(8 + r - j, WIDE), :]
        return smooth

    for r in range(0, ROWS, WIDE):
        mixed = gate[pl.ds(r, WIDE), :].astype(F32) * smooth_rows(r)
        mix_t[:, pl.ds(r, WIDE)] = mixed.T.astype(BF16)
    outs = Scatter(scatter_out, at)
    next(step)

    def multiply(sub, o, first=False):
        m = ring.ready(sub, o)
        cols = pl.ds(pl.multiple_of(m * 2 * WIDE, 2 * WIDE), 2 * WIDE)
        shards = jnp.concatenate([whole_out[2 * m], whole_out[2 * m + 1]], axis=1)
        part = lax.dot_general(
            upstream[:, cols], shards, (((1,), (1,)), ((), ())), preferred_element_type=F32
        )
        acc[...] = part if first else acc[...] + part

    loaded(4)
    multiply(0, 0, True)
    multiply(1, 0)
    outs.partials(product_t, upstream, 0, 1)
    for d in range(2, 5):
        next(step)
        multiply(0, d - 1)
        multiply(0, 1 - d)
        outs.partials(product_t, upstream, 2 * d - 3, 2 * d - 2)
        next(step)
        multiply(1, d - 1)
        multiply(1, 1 - d)
        if d < 4:
            outs.partials(product_t, upstream, 2 * d - 2, 2 * d - 1)
    for _ in step:
        pass
    multiply(0, 4)
    multiply(1, 4)

    for r in range(0, ROWS, WIDE):
        rows = pl.ds(r, WIDE)
        conv = acc[rows, :] * outer_gate[rows, :].astype(F32)
        conv_t[:, rows] = conv.T.astype(BF16)
    exchange(lambda d: conv_t.at[sixteen(d)], conv_rx.at[sixteen(s)], conv_s, conv_r, s)
    conv_rx[sixteen(s), :] = conv_t[sixteen(s), :]
    ring_in = Gather(in_shard, whole_in, sems_in, at)
    ring_in.begin()
    in_step = ring_in.steps()
    exchange(lambda d: mix_t.at[sixteen(d)], mix_rx.at[sixteen(s)], mix_s, mix_r, s)
    mix_rx[sixteen(s), :] = mix_t[sixteen(s), :]
    for r in range(0, ROWS, WIDE):
        rows = pl.ds(r, WIDE)
        grad_outer[rows, :] = (acc[rows, :] * conv_output[rows, :].astype(F32)).astype(BF16)
    loaded(5, *range(7, 15))

    def filter_rows(j, _):
        other_f[sixteen(j), :] = filters[:, lanes_at(j)].astype(F32)
        return 0

    lax.fori_loop(0, OUTER, filter_rows, 0)
    spectra = Spectra(tables)

    def take_filter(i, _):
        spec_h[i] = spectra.forward(other_f, i)
        return 0

    lax.fori_loop(0, 4, take_filter, 0)
    next(in_step)
    lax.fori_loop(4, 8, take_filter, 0)
    outs.partials(product_t, upstream, 6, 8)
    out_step = outs.steps()
    next(in_step)

    arrived(lambda d: conv_rx.at[sixteen(d)], conv_s, conv_r, s)
    spread(conv_rx, conv_f)

    def take_mixed(i, _):
        spec = spectra.forward(conv_f, i)
        spec_g[i] = spec
        spectra.inverse(spec, spec_h[i], out_f, i)
        return 0

    lax.fori_loop(0, 3, take_mixed, 0)
    next(in_step)
    lax.fori_loop(3, 6, take_mixed, 0)
    next(in_step)
    lax.fori_loop(6, 8, take_mixed, 0)

    def gather_rows(n, _):
        for q in range(3):
            mixed_cols[sixteen(n), q * WIDE : (q + 1) * WIDE] = out_f[
                sixteen(3 * n + q), :
            ].astype(BF16)
        return 0

    lax.fori_loop(0, N_SEQ, gather_rows, 0)
    exchange(lambda d: mixed_cols.at[sixteen(d)], mixed_rx.at[sixteen(s)], back_s, back_r, s)
    mixed_rx[sixteen(s), :] = mixed_cols[sixteen(s), :]

    arrived(lambda d: mix_rx.at[sixteen(d)], mix_s, mix_r, s)
    spread(mix_rx, other_f)

    def take_long(i, _):
        spectra.inverse(spec_g[i], spectra.forward(other_f, i), out_f, i)
        return 0

    lax.fori_loop(0, 2, take_long, 0)
    next(in_step)
    lax.fori_loop(2, 5, take_long, 0)
    next(in_step)
    lax.fori_loop(5, 8, take_long, 0)
    next(in_step)

    arrived(lambda d: mixed_rx.at[sixteen(d)], back_s, back_r, s)

    edge_back = remote(
        grads.at[pl.ds(0, 8)],
        halo_back,
        halo_sem.at[2],
        halo_sem.at[3],
        "seq",
        (s + N_SEQ - 1) % N_SEQ,
    )
    for r in range(0, ROWS, WIDE):
        rows = pl.ds(r, WIDE)
        mixed = mixed_rx[:, rows].astype(F32).T
        grads[rows, :] = mixed * gate[rows, :].astype(F32)
        if r == 0:
            edge_back.start()
        grad_inner[rows, :] = (mixed * smooth_rows(r)).astype(BF16)
    edge_back.wait_recv()
    grads[pl.ds(ROWS, 8), :] = jnp.where(s == N_SEQ - 1, 0.0, halo_back[...])
    for r in range(0, ROWS, WIDE):
        rows = pl.ds(r, WIDE)
        out = all_taps[pl.ds(0, 1), :] * grads[rows, :]
        for j in range(1, 3):
            out = out + all_taps[pl.ds(j, 1), :] * grads[pl.ds(r + j, WIDE), :]
        value[rows, :] = out.astype(BF16)
        value_t[:, rows] = out.T.astype(BF16)

    for _ in in_step:
        pass
    for sub in range(2):
        for o in range(-3, 5):
            ring_in.ready(sub, o)

    def part_of(sub, o):
        n = (1 - low if sub else low) * 4 + (x + o + 4) % 4
        w = jnp.concatenate([whole_in[4 * n + i] for i in range(4)], axis=0)
        acc[...] = lax.dot_general(
            value[...], w, (((1,), (1,)), ((), ())), preferred_element_type=F32
        )

    def x_hop(di, d, sub):
        return remote(
            x_own.at[sub, (SIGNS[di] * d) % 4],
            x_rx.at[di, d - 1, sub],
            x_s.at[di, d - 1, sub],
            x_r.at[di, d - 1, sub],
            "ch",
            low * 4 + (x + SIGNS[di] + 4) % 4,
        )

    hops = []

    def x_go(di, d, sub):
        o = (SIGNS[di] * d) % 4
        part_of(sub, o)
        value_out = acc[...]
        if d == 1 and sub == di:
            x_hop(di, 2, sub).wait_recv()
            value_out = value_out + x_rx[di, 1, sub].astype(F32)
        x_own[sub, o] = value_out.astype(BF16)
        hop = x_hop(di, d, sub)
        hop.start()
        hops.append(hop)

    def x_total(sub):
        part_of(sub, 0)
        value_out = acc[...]
        for di in range(2):
            x_hop(di, 1, sub).wait_recv()
            value_out = value_out + x_rx[di, 0, sub].astype(F32)
        return value_out

    partner = remote(y_io.at[0], y_io.at[1], p_s.at[0], p_s.at[1], "ch", (1 - low) * 4 + x)

    x_go(0, 2, 0)
    x_go(1, 2, 1)
    next(out_step)
    next(out_step)
    loaded(6)
    total = Scatter(scatter_in, at)
    total.partials(value_t, layer_input, 0, 2)
    step = total.steps()
    next(step)
    next(step)
    total.partials(value_t, layer_input, 2, 5)
    next(out_step)
    x_go(0, 1, 1)
    total.partials(value_t, layer_input, 5, 8)
    next(step)

    sums = []
    for j in range(3):
        part = jnp.zeros((1, CHANS), F32)
        for r in range(0, ROWS, WIDE):
            part = part + jnp.sum(
                grads[pl.ds(r, WIDE), :] * padded[pl.ds(8 + r - j, WIDE), :], axis=0, keepdims=True
            )
        sums.append(part)
    short_tx[...] = jnp.concatenate(sums + [jnp.zeros((5, CHANS), F32)], axis=0)
    exchange(lambda d: short_tx.at[:, lanes_at(d // 8)], short_rx.at[s], short_s, short_r, s)
    short_rx[s] = short_tx[:, lanes_at(s // 8)]

    x_go(1, 1, 1)
    next(step)
    next(out_step)

    def long_rows(j, _):
        grad_long[:, lanes_at(j)] = out_f[sixteen(j), :]
        return 0

    lax.fori_loop(0, OUTER, long_rows, 0)
    x_go(1, 1, 0)
    next(step)
    next(out_step)
    x_go(0, 1, 0)
    next(step)
    next(out_step)
    next(step)
    for _ in out_step:
        pass
    for _ in step:
        pass
    y_io[0] = x_total(1).astype(BF16)
    partner.start()
    outs.finish(grad_outproj)
    total.finish(inproj_t)
    grad_inproj[...] = inproj_t[...].T
    arrived(lambda d: short_rx.at[d], short_s, short_r, s)
    tile = short_rx[0]
    for i in range(1, N_SEQ):
        tile = tile + short_rx[i]
    grad_short[...] = tile
    edge_back.wait_send()
    grads[pl.ds(0, ROWS), :] = x_total(0)
    partner.wait_recv()
    grad_input[...] = (grads[pl.ds(0, ROWS), :] + y_io[1].astype(F32)).astype(BF16)

    for hop in hops:
        hop.wait_send()
    partner.wait_send()
    edge.wait_send()
    ring.end()
    ring_in.end()

    left(taps, taps_s, taps_r, s)
    left(mix_t.at[sixteen(0)], mix_s, mix_r, s)
    left(conv_t.at[sixteen(0)], conv_s, conv_r, s)
    left(mixed_cols.at[sixteen(0)], back_s, back_r, s)
    left(short_rx.at[0], short_s, short_r, s)


def hand_out(*refs):
    n = (len(refs) - 1) // 3
    sems = refs[-1]
    inward = [pltpu.make_async_copy(refs[i], refs[2 * n + i], sems.at[i]) for i in range(n)]
    outward = [
        pltpu.make_async_copy(refs[2 * n + i], refs[n + i], sems.at[n + i]) for i in range(n)
    ]
    for copy in inward:
        copy.start()
    for i in range(n):
        inward[i].wait()
        outward[i].start()
    for copy in outward:
        copy.wait()


def shards(
    layer_input, value_proj, outer_gate, inner_gate, conv_output,
    upstream, in_weight, out_weight, long_filter, short_filter,
):
    s = lax.axis_index("seq")
    dma = pltpu.SemaphoreType.DMA
    peers = dma((N_SEQ,))
    vmem = pltpu.VMEM
    lane = ((s % 8) * MINE).astype(jnp.int32)
    taps = lax.dynamic_update_slice(
        jnp.zeros((8, WIDE), F32), short_filter[0].T, (jnp.int32(0), lane)
    )
    tables = [jnp.asarray(t) for t in dft_tables()]
    outs = [
        jax.ShapeDtypeStruct(shape, dtype)
        for shape, dtype in (
            ((ROWS, CHANS), BF16),
            ((ROWS, CHANS), BF16),
            ((ROWS, CHANS), BF16),
            ((MINE, LENGTH), F32),
            ((8, WIDE), F32),
            ((WIDE, CHANS), F32),
            ((CHANS, WIDE), F32),
        )
    ]
    args = (
        layer_input, value_proj, outer_gate, inner_gate, conv_output, upstream, in_weight, out_weight,
        long_filter[0], taps, *tables,
    )
    local = [vmem((ROWS, CHANS), BF16)] * 4
    block = vmem((CHANS, ROWS), BF16)
    signal = vmem((MINE * OUTER, WIDE), F32)
    spectrum = vmem((MINE // 2, 2 * OUTER, 2 * WIDE), F32)
    scratch = [
        vmem((ROWS, DEEP), BF16),
        *local,
        vmem((ROWS, DEEP), BF16),
        vmem((MINE, LENGTH), BF16),
        *[vmem(t.shape, t.dtype) for t in tables],
        vmem((N_SEQ, CHANS, WIDE), BF16),
        vmem((N_SEQ, WIDE, CHANS), BF16),
        vmem((ROWS, CHANS), F32),
        *[block] * 7,
        vmem((ROWS, CHANS), BF16),
        block,
        vmem((2, 4, ROWS, CHANS), BF16),
        vmem((2, 2, 2, ROWS, CHANS), BF16),
        vmem((2, ROWS, CHANS), BF16),
        vmem((ROWS + 8, CHANS), F32),
        vmem((8, CHANS), F32),
        vmem((16, CHANS), BF16),
        vmem((N_SEQ, 8, WIDE), F32),
        vmem((ROWS + 8, CHANS), F32),
        vmem((8, CHANS), F32),
        vmem((8, CHANS), F32),
        vmem((N_SEQ, 8, WIDE), F32),
        signal, signal, signal, spectrum, spectrum,
        vmem((CHANS, WIDE), F32),
        dma((16,)), dma((5,)),
        *[peers] * 10,
        dma((2, 2, 2)), dma((2, 2, 2)), dma((2,)),
        *Gather.sems, *Gather.sems, *Scatter.scratch(), *Scatter.scratch(),
    ]
    results = pl.pallas_call(
        whole_kernel,
        out_shape=outs,
        in_specs=[pl.BlockSpec(memory_space=pl.ANY)] * len(args),
        out_specs=[pl.BlockSpec(memory_space=pltpu.VMEM)] * len(outs),
        scratch_shapes=scratch,
        compiler_params=pltpu.CompilerParams(
            collective_id=0, has_side_effects=True, vmem_limit_bytes=60 * 2**20
        ),
        cost_estimate=pl.CostEstimate(
            flops=12 * 10**9, bytes_accessed=20 * 2**20, transcendentals=0
        ),
    )(*args)
    (
        grad_input, grad_outer, grad_inner, grad_long, grad_short, grad_inproj, grad_outproj,
    ) = pl.pallas_call(
        hand_out,
        out_shape=outs,
        in_specs=[pl.BlockSpec(memory_space=pl.ANY)] * len(outs),
        out_specs=[pl.BlockSpec(memory_space=pl.ANY)] * len(outs),
        scratch_shapes=[*[vmem(o.shape, o.dtype) for o in outs], dma((2 * len(outs),))],
    )(*results)
    grad_taps = lax.dynamic_slice(grad_short, (jnp.int32(0), lane), (3, MINE)).T
    return (
        grad_input,
        grad_outer,
        grad_inner,
        grad_long[None],
        grad_taps[None],
        grad_inproj,
        grad_outproj,
    )


def solution(mesh):
    in_specs = (
        P("seq", None),
        P("seq", "ch"),
        P("seq", "ch"),
        P("seq", "ch"),
        P("seq", "ch"),
        P("seq", None),
        P("seq", "ch"),
        P("ch", "seq"),
        P("ch", "seq", None),
        P("ch", "seq", None),
    )
    out_specs = (
        P("seq", "ch"),
        P("seq", "ch"),
        P("seq", "ch"),
        P("ch", "seq", None),
        P("ch", "seq", None),
        P("seq", "ch"),
        P("ch", "seq"),
    )
    return jax.shard_map(shards, mesh=mesh, in_specs=in_specs, out_specs=out_specs, check_vma=False)
```

time: 205 us -> 163 us (0.80)
  Pallas kernels: 180 us -> 157 us
  local copies, waits for them, and re-layouts: 13.2 us -> 3 us
  starting transfers between devices: 8.86 us -> 0 us
    pallas_call x3 -> x2, Pallas kernels: 180 us -> 157 us  [the longest x1 154 us: shards(): pl.pallas_call(whole_kernel, out_shape=outs, in_specs=[pl.BlockSpec(memor...]
    ppermute x1 -> x0, starting transfers between devices: 8.86 us -> none  [shards(): in_piece = lax.ppermute(in_weight, ('seq', 'ch'), turned)]
    unnamed x35 -> x4, local copies, waits for them, and re-layouts: 9.96 us -> 1.84 us
  transfers between devices with their start and end apart: 1 -> 0, of which waited for: 0 -> 0; matrix products, arithmetic and copies ran while one was open for 1% -> 0% of each run, Pallas kernels for 29% -> 0%
where the time goes in v2:
time: 163 us; the launch traced here: 161 us
  Pallas kernels  157 us (96%)
  local copies, waits for them, and re-layouts  3 us (2%)
    pallas_call x1, Pallas kernels, shards(): pl.pallas_call(whole_kernel, out_shape=outs, in_specs=[pl.BlockSpec(memor...  154 us

profile of v2, /device:TPU:15, one launch (start us, length us, event | category | flops | bytes accessed | tf_op | source)
XLA Modules:
  0.0 160.5 jit_solution(10572632174988353376)
XLA Ops:
  0.6 0.7 copy.28
  1.3 0.4 dynamic_update_slice.3.refs_9_
  1.7 0.0 copy-start
  1.7 0.6 copy-done
  2.3 154.2 %shard_map.225 = (bf16[384,512]{1,0:T(8,128)(2,1)}, bf16[384,512]{1,0:T(8,128)(2,1)}, bf16[384,512]{1,0:T(8,128)(2,1)}, f32[16,12288]{1,0:T(8,128)}, f32[8,128]{...) custom-call(bf16[384,4096]{1,0:T(8,128)(2,1)} %refs_0_.1, bf16[384,512]{1,0:T(8,128)(2,1)} %refs_1_.1, ...), custom_call_target="tpu_custom_call" | custom-call | flops 12000000000 | bytes 20971520 | tf_op jit(solution)/shard_map/pallas_call | solution.py:876
  156.5 2.7 %shard_map.226 = (bf16[384,512]{1,0:T(8,128)(2,1)}, bf16[384,512]{1,0:T(8,128)(2,1)}, bf16[384,512]{1,0:T(8,128)(2,1)}, f32[16,12288]{1,0:T(8,128)}, f32[8,128]{...) custom-call(bf16[384,512]{1,0:T(8,128)(2,1)} %get-tuple-element.21.refs_0_, ...), custom_call_target="tpu_custom_call" | custom-call | tf_op jit(solution)/shard_map/pallas_call | solution.py:891
  159.2 0.8 dynamic-slice_bitcast_fusion
  160.0 0.6 copy.25
  (1 shorter events, 0.0 us)
Async XLA Ops:
  1.7 0.6 copy-start

commit v3 on v2

--- a/solution.py
+++ b/solution.py
@@ -120,17 +120,22 @@
     lax.fori_loop(1, N_SEQ, body, 0)
 
 
+OVER_Y = (0, 3, 5, 4)
+EARLY_Y = (0, 1, 7, 4)
+
+
 class Gather:
     sems = [
         pltpu.SemaphoreType.DMA((2, 4, 2)),
         pltpu.SemaphoreType.DMA((2, 4, 2)),
         pltpu.SemaphoreType.DMA((2, 8)),
         pltpu.SemaphoreType.DMA((2, 8)),
-        pltpu.SemaphoreType.DMA((3,)),
+        pltpu.SemaphoreType.DMA((9,)),
     ]
 
     def __init__(self, shard, whole, sems, at):
         self.shard, self.whole, self.at = shard, whole, at
+        self.half = shard.shape[0] // 2
         self.zs, self.zr, self.cs, self.cr, self.ys = sems
         self.started = []
 
@@ -151,17 +156,28 @@
     def hop(self, di, d, sub):
         _, y, z, c = self.at
         o = -SIGNS[di] * (d - 1)
-        there = at_seq(y, (z + SIGNS[di] + 8) % 8, c)
+        src, dst = self.source(sub, o), self.whole.at[self.slot(sub, o)]
+        if d == 4:
+            rows = pl.ds(di * self.half, self.half)
+            src = dst = self.whole.at[self.slot(sub, o), rows]
         self.go(
             remote(
-                self.source(sub, o),
-                self.whole.at[self.slot(sub, o)],
+                src,
+                dst,
                 self.zs.at[di, d - 1, sub],
                 self.zr.at[di, d - 1, sub],
                 "seq",
-                there,
+                at_seq(y, (z + SIGNS[di] + 8) % 8, c),
             )
         )
+
+    def landed(self, di, d, sub):
+        here = self.whole.at[self.slot(sub, -SIGNS[di] * d)]
+        if d == 4:
+            here = self.whole.at[self.slot(sub, 4), pl.ds(di * self.half, self.half)]
+        remote(
+            here, here, self.zs.at[di, d - 1, sub], self.zr.at[di, d - 1, sub], "seq", self.at[0]
+        ).wait_recv()
 
     def share(self, sub, o):
         _, y, z, c = self.at
@@ -176,56 +192,71 @@
             )
         )
 
-    def pair(self):
+    def over_y(self, n):
         _, y, z, c = self.at
-        return remote(
-            self.shard,
-            self.whole.at[self.slot(0, 0)],
-            self.ys.at[0],
-            self.ys.at[1],
-            "seq",
-            at_seq(1 - y, z, c),
-        )
-
-    @staticmethod
-    def travels(di, d, sub):
-        return d < 4 or (d == 4 and sub == di)
+        self.go(
+            remote(
+                self.source(0, EARLY_Y[n]),
+                self.whole.at[self.slot(0, EARLY_Y[n])],
+                self.ys.at[2 * n],
+                self.ys.at[2 * n + 1],
+                "seq",
+                at_seq(1 - y, z, c),
+            )
+        )
+
+    def from_y(self, n):
+        here = self.whole.at[self.slot(1, EARLY_Y[n])]
+        remote(
+            here, here, self.ys.at[2 * n], self.ys.at[2 * n + 1], "seq", self.at[0]
+        ).wait_recv()
+        self.share(1, EARLY_Y[n])
 
     def begin(self):
         self.hop(0, 1, 0)
         self.hop(1, 1, 0)
-        self.go(self.pair())
+        self.over_y(0)
         self.share(0, 0)
         self.keep = pltpu.make_async_copy(
-            self.shard, self.whole.at[self.slot(0, 0)], self.ys.at[2]
+            self.shard, self.whole.at[self.slot(0, 0)], self.ys.at[8]
         )
         self.keep.start()
 
+    def serve(self, d, sub, on):
+        for di in range(2):
+            self.landed(di, d, sub)
+            if on:
+                self.hop(di, d + 1, sub)
+        for di in range(2):
+            if d < 4:
+                self.share(sub, -SIGNS[di] * d)
+
     def steps(self):
-        self.pair().wait_recv()
-        self.hop(0, 1, 1)
-        self.hop(1, 1, 1)
-        self.share(1, 0)
+        self.serve(1, 0, True)
+        self.over_y(1)
+        self.over_y(2)
         yield
-        for d in range(1, 5):
-            for sub in range(2):
-                for di in range(2):
-                    if not self.travels(di, d, sub):
-                        continue
-                    o = -SIGNS[di] * d
-                    here = self.whole.at[self.slot(sub, o)]
-                    remote(
-                        here,
-                        here,
-                        self.zs.at[di, d - 1, sub],
-                        self.zr.at[di, d - 1, sub],
-                        "seq",
-                        self.at[0],
-                    ).wait_recv()
-                    if self.travels(di, d + 1, sub):
-                        self.hop(di, d + 1, sub)
-                    self.share(sub, o)
-                yield
+        self.from_y(0)
+        yield
+        self.serve(2, 0, True)
+        yield
+        self.from_y(1)
+        self.hop(1, 2, 1)
+        self.from_y(2)
+        self.hop(0, 2, 1)
+        yield
+        self.serve(3, 0, True)
+        yield
+        self.serve(2, 1, True)
+        yield
+        self.serve(4, 0, False)
+        self.over_y(3)
+        self.share(0, 4)
+        yield
+        self.serve(3, 1, False)
+        yield
+        self.from_y(3)
+        yield
 
     def ready(self, sub, o):
         _, y, z, c = self.at
@@ -251,12 +282,12 @@
             pltpu.VMEM((2, 8, CHANS, WIDE), BF16),
             pltpu.VMEM((2, 8, CHANS, WIDE), BF16),
             pltpu.VMEM((2, 4, 2, CHANS, WIDE), BF16),
-            pltpu.VMEM((2, CHANS, WIDE), BF16),
+            pltpu.VMEM((4, CHANS, WIDE), BF16),
             pltpu.SemaphoreType.DMA((2, 4, 2)),
             pltpu.SemaphoreType.DMA((2, 4, 2)),
             pltpu.SemaphoreType.DMA((2, 8)),
             pltpu.SemaphoreType.DMA((2, 8)),
-            pltpu.SemaphoreType.DMA((2,)),
+            pltpu.SemaphoreType.DMA((8,)),
         ]
 
     def __init__(self, scratch, at):
@@ -305,23 +336,27 @@
     def hop(self, di, d, sub):
         _, y, z, c = self.at
         o = (SIGNS[di] * d) % 8
-        there = at_seq(y, (z + SIGNS[di] + 8) % 8, c)
+        src, dst = self.own.at[sub, o], self.zrx.at[di, d - 1, sub]
+        if d == 4:
+            half = CHANS // 2
+            src = self.own.at[sub, o, pl.ds(di * half, half)]
+            dst = self.zrx.at[di, d - 1, sub, pl.ds(0, half)]
         return remote(
-            self.own.at[sub, o],
-            self.zrx.at[di, d - 1, sub],
+            src,
+            dst,
             self.zs.at[di, d - 1, sub],
             self.zr.at[di, d - 1, sub],
             "seq",
-            there,
-        )
-
-    def pair(self):
+            at_seq(y, (z + SIGNS[di] + 8) % 8, c),
+        )
+
+    def over_y(self, n):
         _, y, z, c = self.at
         return remote(
-            self.yrx.at[0],
-            self.yrx.at[1],
-            self.ys.at[0],
-            self.ys.at[1],
+            self.own.at[1, OVER_Y[n]],
+            self.yrx.at[n],
+            self.ys.at[2 * n],
+            self.ys.at[2 * n + 1],
             "seq",
             at_seq(1 - y, z, c),
         )
@@ -330,35 +365,56 @@
         self.hand(sub, o).wait_recv()
         return self.own[sub, o].astype(F32) + self.rx[sub, o].astype(F32)
 
+    def with_y(self, n):
+        total = self.both(0, OVER_Y[n])
+        self.over_y(n).wait_recv()
+        return total + self.yrx[n].astype(F32)
+
     def steps(self):
-        for d in range(4, 0, -1):
-            for sub in range(2):
-                for di in range(2):
-                    if not Gather.travels(di, d, sub):
-                        continue
-                    o = (SIGNS[di] * d) % 8
+        for n in (3, 1, 2):
+            o = OVER_Y[n]
+            self.own[1, o] = self.both(1, o).astype(BF16)
+            self.go(self.over_y(n))
+        yield
+        self.own[0, 4] = self.with_y(3).astype(BF16)
+        self.go(self.hop(0, 4, 0))
+        self.go(self.hop(1, 4, 0))
+        yield
+        half = CHANS // 2
+        for d, sub in ((2, 1), (3, 0), (1, 1), (2, 0), (0, 1), (1, 0)):
+            if d == 0:
+                self.own[1, 0] = self.ended(1).astype(BF16)
+                self.go(self.over_y(0))
+                yield
+                continue
+            for di in range(2):
+                o = (SIGNS[di] * d) % 8
+                if d == 3:
+                    total = self.with_y(1 + di)
+                    self.hop(di, 4, 0).wait_recv()
+                    parts = [total[:half], total[half:]]
+                    parts[di] = parts[di] + self.zrx[di, 3, 0, :half].astype(F32)
+                    total = jnp.concatenate(parts, axis=0)
+                else:
                     total = self.both(sub, o)
-                    if Gather.travels(di, d + 1, sub):
+                    if (d, sub) != (2, 1):
                         self.hop(di, d + 1, sub).wait_recv()
                         total = total + self.zrx[di, d, sub].astype(F32)
-                    self.own[sub, o] = total.astype(BF16)
-                    self.go(self.hop(di, d, sub))
-                yield
+                self.own[sub, o] = total.astype(BF16)
+                self.go(self.hop(di, d, sub))
+            yield
+
+    def ended(self, sub):
+        value = self.both(sub, 0)
+        for di in range(2):
+            self.hop(di, 1, sub).wait_recv()
+            value = value + self.zrx[di, 0, sub].astype(F32)
+        return value
 
     def finish(self, out):
-        def total(sub):
-            value = self.both(sub, 0)
-            for di in range(2):
-                self.hop(di, 1, sub).wait_recv()
-                value = value + self.zrx[di, 0, sub].astype(F32)
-            return value
-
-        self.yrx[0] = total(1).astype(BF16)
-        self.pair().start()
-        out[...] = total(0)
-        self.pair().wait_recv()
-        out[...] += self.yrx[1].astype(F32)
-        self.pair().wait_send()
+        out[...] = self.ended(0)
+        self.over_y(0).wait_recv()
+        out[...] += self.yrx[0].astype(F32)
         for copy in self.started:
             copy.wait_send()
 
@@ -460,9 +516,9 @@
     ) = refs[25:40]
     (
         whole_out, whole_in, acc, product_t, conv_t, mix_t, conv_rx, mix_rx, mixed_cols, mixed_rx,
-        value, value_t, x_own, x_rx, y_io, padded, all_taps, halo, taps_rx, grads, halo_back, short_tx, short_rx,
-        conv_f, other_f, out_f, spec_g, spec_h, inproj_t,
-        load_sem, halo_sem, taps_s, taps_r, mix_s, mix_r, conv_s, conv_r,
+        value, value_t, blocks, padded, all_taps, halo, taps_rx, grads, halo_back, short_tx, short_rx,
+        conv_f, other_f, out_f, spec_g, spec_h, in_piece, inproj_t,
+        load_sem, halo_sem, twin_sem, taps_s, taps_r, mix_s, mix_r, conv_s, conv_r,
         back_s, back_r, short_s, short_r, x_s, x_r, p_s,
     ) = refs[40:84]
     rest = refs[84:]
@@ -473,11 +529,17 @@
     s, y, z, c = at
     ch = lax.axis_index("ch")
     x, low = ch % 4, ch // 4
+    twin = {"seq": 4 * ch + s % 4, "ch": s // 4}
+    away = s // 4 != ch
 
     barrier = pltpu.get_barrier_semaphore()
     greet_all(barrier, s)
     for there in (low * 4 + (x + 1) % 4, low * 4 + (x + 3) % 4, (1 - low) * 4 + x):
         pl.semaphore_signal(barrier, inc=1, device_id={"ch": there}, device_id_type=MESH)
+
+    @pl.when(away)
+    def _():
+        pl.semaphore_signal(barrier, inc=1, device_id=twin, device_id_type=MESH)
 
     sources = [outer_hbm, conv_hbm, value_hbm, gate_hbm, up_hbm, filter_hbm, layer_hbm, *table_hbm]
     targets = [outer_gate, conv_output, value_in, gate, upstream, filters, layer_input, *tables]
@@ -491,7 +553,13 @@
         for n in which:
             loads[n].wait()
 
-    pl.semaphore_wait(barrier, N_SEQ - 1 + 3)
+    @pl.when(away)
+    def _():
+        pl.semaphore_wait(barrier, N_SEQ - 1 + 4)
+
+    @pl.when(jnp.logical_not(away))
+    def _():
+        pl.semaphore_wait(barrier, N_SEQ - 1 + 3)
 
     ring = Gather(out_shard, whole_out, sems_out, at)
     ring.begin()
@@ -507,6 +575,18 @@
     exchange(lambda d: taps, taps_rx.at[s], taps_s, taps_r, s)
     taps_own = pltpu.make_async_copy(taps, taps_rx.at[s], halo_sem.at[4])
     taps_own.start()
+    turn = remote_to(in_shard, in_piece, twin_sem.at[0], twin_sem.at[1], twin)
+    stay = pltpu.make_async_copy(in_shard, in_piece, twin_sem.at[2])
+
+    def turn_out():
+        @pl.when(away)
+        def _():
+            turn.start()
+
+        @pl.when(jnp.logical_not(away))
+        def _():
+            stay.start()
+
     step = ring.steps()
     loaded(0, 1)
     for r in range(0, ROWS, WIDE):
@@ -552,21 +632,22 @@
 
     loaded(4)
     multiply(0, 0, True)
-    multiply(1, 0)
+    multiply(0, 1)
+    multiply(0, -1)
     outs.partials(product_t, upstream, 0, 1)
-    for d in range(2, 5):
+    order = ((1, (0,)), (0, (2, -2)), (1, (1, -1)), (0, (3, -3)), (1, (2, -2)), (0, (4,)))
+    for n, (sub, offsets) in enumerate(order):
         next(step)
-        multiply(0, d - 1)
-        multiply(0, 1 - d)
-        outs.partials(product_t, upstream, 2 * d - 3, 2 * d - 2)
-        next(step)
-        multiply(1, d - 1)
-        multiply(1, 1 - d)
-        if d < 4:
-            outs.partials(product_t, upstream, 2 * d - 2, 2 * d - 1)
+        if n == 1:
+            turn_out()
+        for o in offsets:
+            multiply(sub, o)
+        if n < 5:
+            outs.partials(product_t, upstream, n + 1, n + 2)
+    multiply(1, 3)
+    multiply(1, -3)
     for _ in step:
         pass
-    multiply(0, 4)
     multiply(1, 4)
 
     for r in range(0, ROWS, WIDE):
@@ -575,11 +656,18 @@
         conv_t[:, rows] = conv.T.astype(BF16)
     exchange(lambda d: conv_t.at[sixteen(d)], conv_rx.at[sixteen(s)], conv_s, conv_r, s)
     conv_rx[sixteen(s), :] = conv_t[sixteen(s), :]
-    ring_in = Gather(in_shard, whole_in, sems_in, at)
+
+    @pl.when(away)
+    def _():
+        turn.wait_recv()
+
+    @pl.when(jnp.logical_not(away))
+    def _():
+        stay.wait()
+
+    ring_in = Gather(in_piece, whole_in, sems_in, at)
     ring_in.begin()
     in_step = ring_in.steps()
-    exchange(lambda d: mix_t.at[sixteen(d)], mix_rx.at[sixteen(s)], mix_s, mix_r, s)
-    mix_rx[sixteen(s), :] = mix_t[sixteen(s), :]
     for r in range(0, ROWS, WIDE):
         rows = pl.ds(r, WIDE)
         grad_outer[rows, :] = (acc[rows, :] * conv_output[rows, :].astype(F32)).astype(BF16)
@@ -601,9 +689,12 @@
     lax.fori_loop(4, 8, take_filter, 0)
     outs.partials(product_t, upstream, 6, 8)
     out_step = outs.steps()
+    next(out_step)
     next(in_step)
 
     arrived(lambda d: conv_rx.at[sixteen(d)], conv_s, conv_r, s)
+    exchange(lambda d: mix_t.at[sixteen(d)], mix_rx.at[sixteen(s)], mix_s, mix_r, s)
+    mix_rx[sixteen(s), :] = mix_t[sixteen(s), :]
     spread(conv_rx, conv_f)
 
     def take_mixed(i, _):
@@ -629,21 +720,20 @@
     exchange(lambda d: mixed_cols.at[sixteen(d)], mixed_rx.at[sixteen(s)], back_s, back_r, s)
     mixed_rx[sixteen(s), :] = mixed_cols[sixteen(s), :]
 
-    arrived(lambda d: mix_rx.at[sixteen(d)], mix_s, mix_r, s)
-    spread(mix_rx, other_f)
-
     def take_long(i, _):
         spectra.inverse(spec_g[i], spectra.forward(other_f, i), out_f, i)
         return 0
 
-    lax.fori_loop(0, 2, take_long, 0)
     next(in_step)
-    lax.fori_loop(2, 5, take_long, 0)
+    arrived(lambda d: mix_rx.at[sixteen(d)], mix_s, mix_r, s)
+    spread(mix_rx, other_f)
+    lax.fori_loop(0, 3, take_long, 0)
     next(in_step)
-    lax.fori_loop(5, 8, take_long, 0)
+    lax.fori_loop(3, 6, take_long, 0)
     next(in_step)
-
     arrived(lambda d: mixed_rx.at[sixteen(d)], back_s, back_r, s)
+    next(out_step)
+    next(out_step)
 
     edge_back = remote(
         grads.at[pl.ds(0, 8)],
@@ -670,68 +760,56 @@
         value[rows, :] = out.astype(BF16)
         value_t[:, rows] = out.T.astype(BF16)
 
-    for _ in in_step:
-        pass
-    for sub in range(2):
-        for o in range(-3, 5):
-            ring_in.ready(sub, o)
-
-    def part_of(sub, o):
-        n = (1 - low if sub else low) * 4 + (x + o + 4) % 4
-        w = jnp.concatenate([whole_in[4 * n + i] for i in range(4)], axis=0)
-        acc[...] = lax.dot_general(
-            value[...], w, (((1,), (1,)), ((), ())), preferred_element_type=F32
-        )
+    def block(sub, o):
+        return (1 - low if sub else low) * 4 + (x + o + 4) % 4
 
     def x_hop(di, d, sub):
+        o = -SIGNS[di] * (d - 1)
         return remote(
-            x_own.at[sub, (SIGNS[di] * d) % 4],
-            x_rx.at[di, d - 1, sub],
+            value if (sub, o) == (0, 0) else blocks.at[block(sub, o)],
+            blocks.at[block(sub, o)],
             x_s.at[di, d - 1, sub],
             x_r.at[di, d - 1, sub],
             "ch",
             low * 4 + (x + SIGNS[di] + 4) % 4,
         )
 
+    def x_wait(di, d, sub):
+        here = blocks.at[block(sub, -SIGNS[di] * d)]
+        remote(
+            here, here, x_s.at[di, d - 1, sub], x_r.at[di, d - 1, sub], "ch", ch
+        ).wait_recv()
+
+    partner = remote(
+        value, blocks.at[block(0, 0)], p_s.at[0], p_s.at[1], "ch", (1 - low) * 4 + x
+    )
     hops = []
 
     def x_go(di, d, sub):
-        o = (SIGNS[di] * d) % 4
-        part_of(sub, o)
-        value_out = acc[...]
-        if d == 1 and sub == di:
-            x_hop(di, 2, sub).wait_recv()
-            value_out = value_out + x_rx[di, 1, sub].astype(F32)
-        x_own[sub, o] = value_out.astype(BF16)
         hop = x_hop(di, d, sub)
         hop.start()
         hops.append(hop)
 
-    def x_total(sub):
-        part_of(sub, 0)
-        value_out = acc[...]
-        for di in range(2):
-            x_hop(di, 1, sub).wait_recv()
-            value_out = value_out + x_rx[di, 0, sub].astype(F32)
-        return value_out
-
-    partner = remote(y_io.at[0], y_io.at[1], p_s.at[0], p_s.at[1], "ch", (1 - low) * 4 + x)
-
-    x_go(0, 2, 0)
-    x_go(1, 2, 1)
+    x_go(0, 1, 0)
+    x_go(1, 1, 0)
+    partner.start()
     next(out_step)
-    next(out_step)
+    blocks[block(0, 0)] = value[...]
     loaded(6)
     total = Scatter(scatter_in, at)
-    total.partials(value_t, layer_input, 0, 2)
+    total.partials(value_t, layer_input, 0, 3)
     step = total.steps()
     next(step)
+    total.partials(value_t, layer_input, 3, 6)
     next(step)
-    total.partials(value_t, layer_input, 2, 5)
     next(out_step)
+    total.partials(value_t, layer_input, 6, 8)
+    next(step)
+    partner.wait_recv()
     x_go(0, 1, 1)
-    total.partials(value_t, layer_input, 5, 8)
+    x_go(1, 1, 1)
     next(step)
+    next(out_step)
 
     sums = []
     for j in range(3):
@@ -745,29 +823,51 @@
     exchange(lambda d: short_tx.at[:, lanes_at(d // 8)], short_rx.at[s], short_s, short_r, s)
     short_rx[s] = short_tx[:, lanes_at(s // 8)]
 
-    x_go(1, 1, 1)
+    x_wait(0, 1, 0)
+    x_go(0, 2, 0)
+    x_wait(1, 1, 0)
     next(step)
     next(out_step)
+    next(in_step)
+    next(step)
+    next(out_step)
+    next(in_step)
+    x_wait(1, 1, 1)
+    x_go(1, 2, 1)
+    next(step)
+    for _ in out_step:
+        pass
+    for _ in in_step:
+        pass
+    lax.fori_loop(6, 8, take_long, 0)
+    next(step)
 
     def long_rows(j, _):
         grad_long[:, lanes_at(j)] = out_f[sixteen(j), :]
         return 0
 
     lax.fori_loop(0, OUTER, long_rows, 0)
-    x_go(1, 1, 0)
-    next(step)
-    next(out_step)
-    x_go(0, 1, 0)
-    next(step)
-    next(out_step)
-    next(step)
-    for _ in out_step:
-        pass
+    for sub in range(2):
+        for o in range(-3, 5):
+            ring_in.ready(sub, o)
+
+    def finish(n, first=False):
+        w = jnp.concatenate([whole_in[4 * n + i] for i in range(4)], axis=0)
+        part = lax.dot_general(
+            blocks[n], w, (((1,), (1,)), ((), ())), preferred_element_type=F32
+        )
+        acc[...] = part if first else acc[...] + part
+
+    finish(ch, True)
+    finish(block(1, 0))
+    finish(block(0, -1))
+    finish(block(0, 1))
+    finish(block(1, 1))
     for _ in step:
         pass
-    y_io[0] = x_total(1).astype(BF16)
-    partner.start()
     outs.finish(grad_outproj)
+    x_wait(0, 1, 1)
+    finish(block(1, -1))
     total.finish(inproj_t)
     grad_inproj[...] = inproj_t[...].T
     arrived(lambda d: short_rx.at[d], short_s, short_r, s)
@@ -775,10 +875,12 @@
     for i in range(1, N_SEQ):
         tile = tile + short_rx[i]
     grad_short[...] = tile
+    x_wait(0, 2, 0)
+    finish(block(0, 2))
+    x_wait(1, 2, 1)
+    finish(block(1, 2))
+    grad_input[...] = acc[...].astype(BF16)
     edge_back.wait_send()
-    grads[pl.ds(0, ROWS), :] = x_total(0)
-    partner.wait_recv()
-    grad_input[...] = (grads[pl.ds(0, ROWS), :] + y_io[1].astype(F32)).astype(BF16)
 
     for hop in hops:
         hop.wait_send()
@@ -786,6 +888,11 @@
     edge.wait_send()
     ring.end()
     ring_in.end()
+
+    @pl.when(away)
+    def _():
+        turn.wait_send()
+
 
     left(taps, taps_s, taps_r, s)
     left(mix_t.at[sixteen(0)], mix_s, mix_r, s)
@@ -855,9 +962,7 @@
         *[block] * 7,
         vmem((ROWS, CHANS), BF16),
         block,
-        vmem((2, 4, ROWS, CHANS), BF16),
-        vmem((2, 2, 2, ROWS, CHANS), BF16),
-        vmem((2, ROWS, CHANS), BF16),
+        vmem((8, ROWS, CHANS), BF16),
         vmem((ROWS + 8, CHANS), F32),
         vmem((8, CHANS), F32),
         vmem((16, CHANS), BF16),
@@ -867,8 +972,9 @@
         vmem((8, CHANS), F32),
         vmem((N_SEQ, 8, WIDE), F32),
         signal, signal, signal, spectrum, spectrum,
+        vmem((WIDE, CHANS), BF16),
         vmem((CHANS, WIDE), F32),
-        dma((16,)), dma((5,)),
+        dma((16,)), dma((5,)), dma((3,)),
         *[peers] * 10,
         dma((2, 2, 2)), dma((2, 2, 2)), dma((2,)),
         *Gather.sems, *Gather.sems, *Scatter.scratch(), *Scatter.scratch(),

time: 163 us -> 151 us (0.926); the launches traced: 161 us -> 151 us
  Pallas kernels: 157 us -> 148 us
    pallas_call x1, Pallas kernels: 154 us -> 145 us  [shards(): pl.pallas_call(whole_kernel, out_shape=outs, in_specs=[pl.BlockSpec(memor...]
where the time goes in v3:
time: 151 us
  Pallas kernels  148 us (98%)
  local copies, waits for them, and re-layouts  3 us (2%)
    pallas_call x1, Pallas kernels, shards(): pl.pallas_call(whole_kernel, out_shape=outs, in_specs=[pl.BlockSpec(memor...  145 us

profile of v3, /device:TPU:15, one launch (start us, length us, event | category | flops | bytes accessed | tf_op | source)
XLA Modules:
  0.0 151.2 jit_solution(4314645068044649349)
XLA Ops:
  0.6 0.7 copy.28
  1.3 0.4 dynamic_update_slice.3.refs_9_
  1.7 0.0 copy-start
  1.7 0.6 copy-done
  2.3 144.9 %shard_map.225 = (bf16[384,512]{1,0:T(8,128)(2,1)}, bf16[384,512]{1,0:T(8,128)(2,1)}, bf16[384,512]{1,0:T(8,128)(2,1)}, f32[16,12288]{1,0:T(8,128)}, f32[8,128]{...) custom-call(bf16[384,4096]{1,0:T(8,128)(2,1)} %refs_0_.1, bf16[384,512]{1,0:T(8,128)(2,1)} %refs_1_.1, ...), custom_call_target="tpu_custom_call" | custom-call | flops 12000000000 | bytes 20971520 | tf_op jit(solution)/shard_map/pallas_call | solution.py:982
  147.2 2.7 %shard_map.226 = (bf16[384,512]{1,0:T(8,128)(2,1)}, bf16[384,512]{1,0:T(8,128)(2,1)}, bf16[384,512]{1,0:T(8,128)(2,1)}, f32[16,12288]{1,0:T(8,128)}, f32[8,128]{...) custom-call(bf16[384,512]{1,0:T(8,128)(2,1)} %get-tuple-element.21.refs_0_, ...), custom_call_target="tpu_custom_call" | custom-call | tf_op jit(solution)/shard_map/pallas_call | solution.py:997
  149.9 0.8 dynamic-slice_bitcast_fusion
  150.7 0.6 copy.25
  (1 shorter events, 0.0 us)
Async XLA Ops:
  1.7 0.6 copy-start

commit v4 on v3

--- a/solution.py
+++ b/solution.py
@@ -505,7 +505,7 @@
 
 def whole_kernel(*refs):
     (
-        layer_hbm, value_hbm, outer_hbm, gate_hbm, conv_hbm, up_hbm, in_shard, out_shard, filter_hbm, taps,
+        layer_hbm, value_hbm, outer_hbm, gate_hbm, conv_hbm, up_hbm, in_shard, out_shard, filter_hbm, taps_hbm,
         *table_hbm,
     ) = refs[:18]
     (
@@ -517,11 +517,11 @@
     (
         whole_out, whole_in, acc, product_t, conv_t, mix_t, conv_rx, mix_rx, mixed_cols, mixed_rx,
         value, value_t, blocks, padded, all_taps, halo, taps_rx, grads, halo_back, short_tx, short_rx,
-        conv_f, other_f, out_f, spec_g, spec_h, in_piece, inproj_t,
+        conv_f, other_f, out_f, spec_g, spec_h, in_piece, inproj_t, taps_in, taps,
         load_sem, halo_sem, twin_sem, taps_s, taps_r, mix_s, mix_r, conv_s, conv_r,
         back_s, back_r, short_s, short_r, x_s, x_r, p_s,
-    ) = refs[40:84]
-    rest = refs[84:]
+    ) = refs[40:86]
+    rest = refs[86:]
     sems_out, sems_in = rest[:5], rest[5:10]
     scatter_out, scatter_in = rest[10:20], rest[20:30]
 
@@ -541,8 +541,8 @@
     def _():
         pl.semaphore_signal(barrier, inc=1, device_id=twin, device_id_type=MESH)
 
-    sources = [outer_hbm, conv_hbm, value_hbm, gate_hbm, up_hbm, filter_hbm, layer_hbm, *table_hbm]
-    targets = [outer_gate, conv_output, value_in, gate, upstream, filters, layer_input, *tables]
+    sources = [outer_hbm, conv_hbm, value_hbm, gate_hbm, up_hbm, filter_hbm, layer_hbm, *table_hbm, taps_hbm]
+    targets = [outer_gate, conv_output, value_in, gate, upstream, filters, layer_input, *tables, taps_in]
     loads = {}
     for n, (src, dst) in enumerate(zip(sources, targets)):
         copy = pltpu.make_async_copy(src, dst, load_sem.at[n])
@@ -572,9 +572,14 @@
         (s + 1) % N_SEQ,
     )
     edge.start()
+    loaded(15)
+    spots = own_lanes()
+    tap_rows = [
+        jnp.sum(taps_in[:, j : j + 1] * spots, axis=0, keepdims=True) for j in range(3)
+    ]
+    taps[...] = jnp.concatenate(tap_rows + [jnp.zeros((5, WIDE), F32)], axis=0)
     exchange(lambda d: taps, taps_rx.at[s], taps_s, taps_r, s)
-    taps_own = pltpu.make_async_copy(taps, taps_rx.at[s], halo_sem.at[4])
-    taps_own.start()
+    taps_rx[s] = taps[...]
     turn = remote_to(in_shard, in_piece, twin_sem.at[0], twin_sem.at[1], twin)
     stay = pltpu.make_async_copy(in_shard, in_piece, twin_sem.at[2])
 
@@ -599,7 +604,6 @@
     for r in range(0, ROWS, WIDE):
         padded[pl.ds(8 + r, WIDE), :] = value_in[pl.ds(r, WIDE), :].astype(F32)
     arrived(lambda d: taps_rx.at[d], taps_s, taps_r, s)
-    taps_own.wait()
     for g in range(4):
         tile = taps_rx[8 * g]
         for i in range(1, 8):
@@ -901,10 +905,23 @@
     left(short_rx.at[0], short_s, short_r, s)
 
 
+TAPS_AT = 4
+
+
+def own_lanes():
+    lane = (lax.axis_index("seq") % 8) * MINE
+    rows = lax.broadcasted_iota(jnp.int32, (MINE, WIDE), 0)
+    cols = lax.broadcasted_iota(jnp.int32, (MINE, WIDE), 1)
+    return jnp.where(cols == rows + lane, 1.0, 0.0).astype(F32)
+
+
 def hand_out(*refs):
-    n = (len(refs) - 1) // 3
-    sems = refs[-1]
-    inward = [pltpu.make_async_copy(refs[i], refs[2 * n + i], sems.at[i]) for i in range(n)]
+    *refs, tile, sems = refs
+    n = len(refs) // 3
+    inward = [
+        pltpu.make_async_copy(refs[i], tile if i == TAPS_AT else refs[2 * n + i], sems.at[i])
+        for i in range(n)
+    ]
     outward = [
         pltpu.make_async_copy(refs[2 * n + i], refs[n + i], sems.at[n + i]) for i in range(n)
     ]
@@ -912,7 +929,16 @@
         copy.start()
     for i in range(n):
         inward[i].wait()
-        outward[i].start()
+        if i != TAPS_AT:
+            outward[i].start()
+    refs[2 * n + TAPS_AT][...] = lax.dot_general(
+        own_lanes(),
+        tile[...],
+        (((1,), (1,)), ((), ())),
+        precision=lax.Precision.HIGHEST,
+        preferred_element_type=F32,
+    )[:, :3]
+    outward[TAPS_AT].start()
     for copy in outward:
         copy.wait()
 
@@ -921,14 +947,9 @@
     layer_input, value_proj, outer_gate, inner_gate, conv_output,
     upstream, in_weight, out_weight, long_filter, short_filter,
 ):
-    s = lax.axis_index("seq")
     dma = pltpu.SemaphoreType.DMA
     peers = dma((N_SEQ,))
     vmem = pltpu.VMEM
-    lane = ((s % 8) * MINE).astype(jnp.int32)
-    taps = lax.dynamic_update_slice(
-        jnp.zeros((8, WIDE), F32), short_filter[0].T, (jnp.int32(0), lane)
-    )
     tables = [jnp.asarray(t) for t in dft_tables()]
     outs = [
         jax.ShapeDtypeStruct(shape, dtype)
@@ -944,7 +965,7 @@
     ]
     args = (
         layer_input, value_proj, outer_gate, inner_gate, conv_output, upstream, in_weight, out_weight,
-        long_filter[0], taps, *tables,
+        long_filter[0], short_filter[0], *tables,
     )
     local = [vmem((ROWS, CHANS), BF16)] * 4
     block = vmem((CHANS, ROWS), BF16)
@@ -974,11 +995,14 @@
         signal, signal, signal, spectrum, spectrum,
         vmem((WIDE, CHANS), BF16),
         vmem((CHANS, WIDE), F32),
-        dma((16,)), dma((5,)), dma((3,)),
+        vmem((MINE, 3), F32), vmem((8, WIDE), F32),
+        dma((16,)), dma((4,)), dma((3,)),
         *[peers] * 10,
         dma((2, 2, 2)), dma((2, 2, 2)), dma((2,)),
         *Gather.sems, *Gather.sems, *Scatter.scratch(), *Scatter.scratch(),
     ]
+    given = list(outs)
+    given[TAPS_AT] = jax.ShapeDtypeStruct((MINE, 3), F32)
     results = pl.pallas_call(
         whole_kernel,
         out_shape=outs,
@@ -996,18 +1020,21 @@
         grad_input, grad_outer, grad_inner, grad_long, grad_short, grad_inproj, grad_outproj,
     ) = pl.pallas_call(
         hand_out,
-        out_shape=outs,
+        out_shape=given,
         in_specs=[pl.BlockSpec(memory_space=pl.ANY)] * len(outs),
         out_specs=[pl.BlockSpec(memory_space=pl.ANY)] * len(outs),
-        scratch_shapes=[*[vmem(o.shape, o.dtype) for o in outs], dma((2 * len(outs),))],
+        scratch_shapes=[
+            *[vmem(o.shape, o.dtype) for o in given],
+            vmem((8, WIDE), F32),
+            dma((2 * len(outs),)),
+        ],
     )(*results)
-    grad_taps = lax.dynamic_slice(grad_short, (jnp.int32(0), lane), (3, MINE)).T
     return (
         grad_input,
         grad_outer,
         grad_inner,
         grad_long[None],
-        grad_taps[None],
+        grad_short[None],
         grad_inproj,
         grad_outproj,
     )

time: 151 us -> 151 us (level)
  no operation moved by 1% of the time
where the time goes in v4:
time: 151 us
  Pallas kernels  147 us (97%)
  local copies, waits for them, and re-layouts  2.69 us (2%)
    pallas_call x1, Pallas kernels, shards(): pl.pallas_call(whole_kernel, out_shape=outs, in_specs=[pl.BlockSpec(memor...  145 us

profile of v4, /device:TPU:15, one launch (start us, length us, event | category | flops | bytes accessed | tf_op | source)
XLA Modules:
  0.0 150.6 jit_solution(8692935985656131717)
XLA Ops:
  0.6 1.4 copy.28
  2.0 144.5 %shard_map.225 = (bf16[384,512]{1,0:T(8,128)(2,1)}, bf16[384,512]{1,0:T(8,128)(2,1)}, bf16[384,512]{1,0:T(8,128)(2,1)}, f32[16,12288]{1,0:T(8,128)}, f32[8,128]{...) custom-call(bf16[384,4096]{1,0:T(8,128)(2,1)} %refs_0_.1, bf16[384,512]{1,0:T(8,128)(2,1)} %refs_1_.1, ...), custom_call_target="tpu_custom_call" | custom-call | flops 12000000000 | bytes 20971520 | tf_op jit(solution)/shard_map/pallas_call | solution.py:1006
  146.5 2.7 %shard_map.226 = (bf16[384,512]{1,0:T(8,128)(2,1)}, bf16[384,512]{1,0:T(8,128)(2,1)}, bf16[384,512]{1,0:T(8,128)(2,1)}, f32[16,12288]{1,0:T(8,128)}, f32[16,3]{1...) custom-call(bf16[384,512]{1,0:T(8,128)(2,1)} %get-tuple-element.21.refs_0_, ...), custom_call_target="tpu_custom_call" | custom-call | tf_op jit(solution)/shard_map/pallas_call | solution.py:1021
  149.2 1.3 copy.27

commit v5 on v4

--- a/solution.py
+++ b/solution.py
@@ -806,12 +806,14 @@
     next(step)
     total.partials(value_t, layer_input, 3, 6)
     next(step)
-    next(out_step)
     total.partials(value_t, layer_input, 6, 8)
-    next(step)
     partner.wait_recv()
     x_go(0, 1, 1)
     x_go(1, 1, 1)
+    x_wait(0, 1, 0)
+    x_go(0, 2, 0)
+    next(out_step)
+    next(step)
     next(step)
     next(out_step)
 
@@ -827,17 +829,15 @@
     exchange(lambda d: short_tx.at[:, lanes_at(d // 8)], short_rx.at[s], short_s, short_r, s)
     short_rx[s] = short_tx[:, lanes_at(s // 8)]
 
-    x_wait(0, 1, 0)
-    x_go(0, 2, 0)
     x_wait(1, 1, 0)
     next(step)
     next(out_step)
     next(in_step)
     next(step)
+    x_wait(1, 1, 1)
+    x_go(1, 2, 1)
     next(out_step)
     next(in_step)
-    x_wait(1, 1, 1)
-    x_go(1, 2, 1)
     next(step)
     for _ in out_step:
         pass

time: 151 us -> 151 us (level)
  no operation moved by 1% of the time
where the time goes in v5:
time: 151 us
  Pallas kernels  148 us (98%)
  local copies, waits for them, and re-layouts  2.69 us (2%)
    pallas_call x1, Pallas kernels, shards(): pl.pallas_call(whole_kernel, out_shape=outs, in_specs=[pl.BlockSpec(memor...  145 us

profile of v5, /device:TPU:15, one launch (start us, length us, event | category | flops | bytes accessed | tf_op | source)
XLA Modules:
  0.0 151.0 jit_solution(92730892258043251)
XLA Ops:
  0.6 1.4 copy.28
  2.0 145.0 %shard_map.225 = (bf16[384,512]{1,0:T(8,128)(2,1)}, bf16[384,512]{1,0:T(8,128)(2,1)}, bf16[384,512]{1,0:T(8,128)(2,1)}, f32[16,12288]{1,0:T(8,128)}, f32[8,128]{...) custom-call(bf16[384,4096]{1,0:T(8,128)(2,1)} %refs_0_.1, bf16[384,512]{1,0:T(8,128)(2,1)} %refs_1_.1, ...), custom_call_target="tpu_custom_call" | custom-call | flops 12000000000 | bytes 20971520 | tf_op jit(solution)/shard_map/pallas_call | solution.py:1006
  147.0 2.7 %shard_map.226 = (bf16[384,512]{1,0:T(8,128)(2,1)}, bf16[384,512]{1,0:T(8,128)(2,1)}, bf16[384,512]{1,0:T(8,128)(2,1)}, f32[16,12288]{1,0:T(8,128)}, f32[16,3]{1...) custom-call(bf16[384,512]{1,0:T(8,128)(2,1)} %get-tuple-element.21.refs_0_, ...), custom_call_target="tpu_custom_call" | custom-call | tf_op jit(solution)/shard_map/pallas_call | solution.py:1021
  149.7 1.3 copy.27
